TPU v7x, 512 devices: a whole 4x4x16 slice. The times are simulated.
512 devices in a mesh: blk: 128 (over y_lo, x, z), feat: 4 (over y_hi, core).
Axes of the slice: x: 4, y: 4 (y_hi: 2, y_lo: 2; y = y_hi * 2 + y_lo), z: 16, core: 2. Of those that a mesh axis runs over, the one named last changes fastest.
Arguments:
- series: bfloat16 [131072, 2048], P('blk', 'feat'), may hold values from -12 to 12
- scales: bfloat16 [131072], P('blk'), may hold values from 0.69921875 to 1.3984375
- width: float32 [1], replicated, may hold values from 2 to 4
Outputs:
- kernel_same: float32 [131072, 1024], P(('blk', 'feat'))
- kernel_next: float32 [131072, 1024], P(('blk', 'feat'))
- kernel_prev: float32 [131072, 1024], P(('blk', 'feat'))
All inputs are finite; a program needn't handle non-finite values.
Results may differ from a plain program's by a relative error of at most 0.0003.
Values may be sent and summed in bfloat16 or wider, within the bound.
A program may use at most 64 MiB of HBM per device.

v0:
```python
import jax
import jax.numpy as jnp
from jax import lax
from jax.sharding import PartitionSpec as P

LAGS = 24


def passed_along(shard, axis, by):
    size = lax.axis_size(axis)
    return lax.ppermute(shard, axis, [(i, (i + by) % size) for i in range(size)])


def kernel_tile(rows_ext, cols_ext, row_scales, col_scales, width):
    nrows = rows_ext.shape[0] - (LAGS - 1)
    ncols = cols_ext.shape[0] - (LAGS - 1)
    gram = lax.dot_general(
        rows_ext, cols_ext, (((1,), (1,)), ((), ())), preferred_element_type=jnp.float32
    )
    row_sq = jnp.sum(jnp.square(rows_ext.astype(jnp.float32)), axis=1)
    col_sq = jnp.sum(jnp.square(cols_ext.astype(jnp.float32)), axis=1)
    spread = row_sq[:, None] + col_sq[None, :] - 2.0 * gram
    total = spread[LAGS - 1 : LAGS - 1 + nrows, LAGS - 1 : LAGS - 1 + ncols]
    for lag in range(1, LAGS):
        total = (
            total
            + spread[
                LAGS - 1 - lag : LAGS - 1 - lag + nrows, LAGS - 1 - lag : LAGS - 1 - lag + ncols
            ]
        )
    dist = total / (LAGS * rows_ext.shape[1])
    denom = (
        width[0] * row_scales.astype(jnp.float32)[:, None] * col_scales.astype(jnp.float32)[None, :]
    )
    return jnp.exp(-dist / denom)


def per_device(series, scales, width):
    block = series.shape[0]
    share = block // lax.axis_size("feat")
    whole = lax.all_gather(series, "feat", axis=1, tiled=True)
    tail = whole[block - (LAGS - 1) :]
    past = passed_along(tail, "blk", 1)
    own_ext = jnp.concatenate([past, whole], axis=0)
    after, after_scales = passed_along((whole, scales), "blk", -1)
    after_ext = jnp.concatenate([tail, after], axis=0)
    start = lax.axis_index("feat") * share
    row_ext = lax.dynamic_slice_in_dim(own_ext, start, share + LAGS - 1, 0)
    row_scales = lax.dynamic_slice_in_dim(scales, start, share, 0)
    same = kernel_tile(row_ext, own_ext, row_scales, scales, width)
    following = kernel_tile(row_ext, after_ext, row_scales, after_scales, width)
    columns = lax.all_to_all(following, "feat", split_axis=1, concat_axis=0, tiled=True)
    before = passed_along(columns.T, "blk", 1)
    return (same, following, before)


def solution(mesh):
    in_specs = (P("blk", "feat"), P("blk"), P())
    out_specs = (P(("blk", "feat"), None), P(("blk", "feat"), None), P(("blk", "feat"), None))
    return jax.shard_map(
        per_device, mesh=mesh, in_specs=in_specs, out_specs=out_specs, check_vma=False
    )
```

profile of v0, /device:TPU:1, one launch (start us, length us, event | category | flops | bytes accessed | tf_op | source)
XLA Modules:
  0.0 238.0 jit_solution(14978298489186679096)
XLA Ops:
  7.2 0.0 all-gather.2.cloned.1.call-start
  7.2 0.7 all-gather.2.cloned.1.call-update
  7.9 54.2 %all-gather.2.cloned.1.call-done = bf16[1024,2048]{1,0:T(8,128)(2,1)} async-done(((bf16[1024,512]{1,0:T(8,128)(2,1)}), bf16[1024,2048]{1,0:T(8,128)(2,1)}) %all-gather.2.cloned.1.call-update) | async-done | bytes 4194320 | tf_op jit(solution)/shard_map/all_gather | solution.py:41
  62.1 7.8 %collective-permute-start.1 = (bf16[1024,2048]{1,0:T(8,128)(2,1)}, bf16[1024,2048]{1,0:T(8,128)(2,1)}, u32[]{:S(2)}, u32[]{:S(2)}) collective-permute-start(bf16[1024,2048]{1,0:T(8,128)(2,1)} %all-gather.2.cloned.1.call-done), channel_id=1, source_target_pairs={{0,508},{4,0},{8,4},{12,8},{16,12},{20,16},{24,20},{28,24},{32,28}... | collective-permute-start | bytes 12582920 | tf_op jit(solution)/shard_map/ppermute | solution.py:11
  69.9 3.0 %collective-permute-start.2 = (bf16[1024]{0:T(1024)(128)(2,1)}, bf16[1024]{0:T(1024)(128)(2,1)S(1)}, u32[]{:S(2)}, u32[]{:S(2)}) collective-permute-start(bf16[1024]{0:T(1024)(128)(2,1)} %param.4), channel_id=1, source_target_pairs={{0,508},{4,0},{8,4},{12,8},{16,12},{20,16},{24,20},{28,24},{32,28}... | collective-permute-start | bytes 6152 | tf_op jit(solution)/shard_map/ppermute | solution.py:11
  73.6 0.9 slice.196
  74.5 2.3 collective-permute-start
  76.8 0.8 convert_multiply_fusion
  77.5 82.4 %collective-permute-done.2 = bf16[1024]{0:T(1024)(128)(2,1)S(1)} collective-permute-done((bf16[1024]{0:T(1024)(128)(2,1)}, bf16[1024]{0:T(1024)(128)(2,1)S(1)}, u32[]{:S(2)}, u32[]{:S(2)}) %collective-permute-start.2) | collective-permute-done | bytes 2080 | tf_op jit(solution)/shard_map/ppermute | solution.py:11
  159.9 1.9 multiply_reduce_fusion.2
  161.8 4.3 %multiply_reduce_fusion = f32[1047]{0:T(1024)S(1)} fusion(bf16[1024,2048]{1,0:T(8,128)(2,1)} %collective-permute-done.1, bf16[23,2048]{1,0:T(8,128)(2,1)S(1)} %slice.196), kind=kLoop, calls=%fused_computation | loop fusion | flops 12864489 | bytes 4292700 | tf_op jit(solution)/shard_map/reduce_sum | solution.py:21
  166.1 3.9 %add_subtract_fusion = f32[279,1047]{1,0:T(8,128)S(1)} fusion(f32[1047]{0:T(1024)S(1)} %multiply_reduce_fusion, bf16[279,2048]{1,0:T(8,128)(2,1)S(1)} %get-tuple-element.4, bf16[1024,2048]{1,0:T(8,128)(2,1)} %collective-permute-done.1, bf16[23,2048]{1,0:T(8,128)(2,1)S(1)} %slice.196, f32[279]{0:T(512)S(1)} %get-tuple-element.3), kind=kOutput, calls=%fused_computation.9 | convolution fusion | flops 1205948160 | bytes 6605052 | tf_op jit(solution)/shard_map/dot_general | solution.py:17
  170.0 8.0 %fusion.4 = f32[256,1024]{1,0:T(8,128)S(1)} fusion(f32[279,1047]{1,0:T(8,128)S(1)} %add_subtract_fusion, f32[1024]{0:T(1024)S(1)} %convert_element_type.25, f32[256]{0:T(256)S(1)} %convert_multiply_fusion), kind=kLoop, calls=%fused_computation.17 | loop fusion | flops 7077888 | bytes 26219520 | tf_op jit(solution)/shard_map/exp | solution.py:35
  178.0 0.0 copy-start.1
  178.0 1.2 copy.11
  179.2 4.6 %all-to-all-start = ((f32[256,4,256]{2,0,1:T(8,128)}), f32[256,4,256]{2,0,1:T(8,128)S(1)}, u32[]{:S(2)}, u32[]{:S(2)}) async-start(f32[256,4,256]{2,0,1:T(8,128)} %bitcast.10), calls=%async_computation | async-start | bytes 2097152 | tf_op jit(solution)/shard_map/all_to_all | solution.py:52
  183.8 4.0 %multiply_reduce_fusion.1 = f32[1047]{0:T(1024)S(1)} fusion(bf16[1024,2048]{1,0:T(8,128)(2,1)} %all-gather.2.cloned.1.call-done, bf16[23,2048]{1,0:T(8,128)(2,1)S(1)} %collective-permute-done), kind=kLoop, calls=%fused_computation.1 | loop fusion | flops 12864489 | bytes 4292700 | tf_op jit(solution)/shard_map/reduce_sum | solution.py:21
  187.8 3.0 %add_subtract_fusion.1 = f32[279,1047]{1,0:T(8,128)S(1)} fusion(bf16[279,2048]{1,0:T(8,128)(2,1)} %copy-done.2, bf16[23,2048]{1,0:T(8,128)(2,1)S(1)} %collective-permute-done, bf16[1024,2048]{1,0:T(8,128)(2,1)S(1)} %copy-done, f32[1047]{0:T(1024)S(1)} %multiply_reduce_fusion.1, f32[279]{0:T(512)S(1)} %get-tuple-element.3), kind=kOutput, calls=%fused_computation.10 | convolution fusion | flops 1205948160 | bytes 6605052 | tf_op jit(solution)/shard_map/dot_general | solution.py:17
  190.8 8.1 %all-to-all-done = f32[256,4,256]{2,0,1:T(8,128)S(1)} async-done(((f32[256,4,256]{2,0,1:T(8,128)}), f32[256,4,256]{2,0,1:T(8,128)S(1)}, u32[]{:S(2)}, u32[]{:S(2)}) %all-to-all-start) | async-done | bytes 1048608 | tf_op jit(solution)/shard_map/all_to_all | solution.py:52
  198.9 0.3 copy.8
  199.2 1.9 collective-permute-start.3
  201.2 8.8 %fusion.8 = f32[256,1024]{1,0:T(8,128)} fusion(f32[279,1047]{1,0:T(8,128)S(1)} %add_subtract_fusion.1, f32[1024]{0:T(1024)S(1)} %convert_element_type.23, f32[256]{0:T(256)S(1)} %convert_multiply_fusion), kind=kLoop, calls=%fused_computation.44 | loop fusion | flops 7077888 | bytes 26219520 | tf_op jit(solution)/shard_map/exp | solution.py:35
  210.0 20.2 %collective-permute-done.3 = f32[256,1024]{1,0:T(8,128)S(1)} collective-permute-done((f32[256,1024]{1,0:T(8,128)S(1)}, f32[256,1024]{1,0:T(8,128)S(1)}, u32[]{:S(2)}, u32[]{:S(2)}) %collective-permute-start.3) | collective-permute-done | bytes 1048608 | tf_op jit(solution)/shard_map/ppermute | solution.py:11
  230.2 1.0 copy.14
  (11 shorter events, 0.0 us)
Async XLA Ops:
  7.2 54.9 %all-gather.2.cloned.1.call-start = ((), (), s32[]{:S(2)}) async-start(), calls=%async_computation.1 | async-start | bytes 5242880 | tf_op jit(solution)/shard_map/all_gather | solution.py:41
  62.1 99.7 %collective-permute-start.1 = (bf16[1024,2048]{1,0:T(8,128)(2,1)}, bf16[1024,2048]{1,0:T(8,128)(2,1)}, u32[]{:S(2)}, u32[]{:S(2)}) collective-permute-start(bf16[1024,2048]{1,0:T(8,128)(2,1)} %all-gather.2.cloned.1.call-done), channel_id=1, source_target_pairs={{0,508},{4,0},{8,4},{12,8},{16,12},{20,16},{24,20},{28,24},{32,28}... | collective-permute-start | bytes 12582920 | tf_op jit(solution)/shard_map/ppermute | solution.py:11
  69.9 90.0 %collective-permute-start.2 = (bf16[1024]{0:T(1024)(128)(2,1)}, bf16[1024]{0:T(1024)(128)(2,1)S(1)}, u32[]{:S(2)}, u32[]{:S(2)}) collective-permute-start(bf16[1024]{0:T(1024)(128)(2,1)} %param.4), channel_id=1, source_target_pairs={{0,508},{4,0},{8,4},{12,8},{16,12},{20,16},{24,20},{28,24},{32,28}... | collective-permute-start | bytes 6152 | tf_op jit(solution)/shard_map/ppermute | solution.py:11
  74.5 85.4 %collective-permute-start = (bf16[23,2048]{1,0:T(8,128)(2,1)S(1)}, bf16[23,2048]{1,0:T(8,128)(2,1)S(1)}, u32[]{:S(2)}, u32[]{:S(2)}) collective-permute-start(bf16[23,2048]{1,0:T(8,128)(2,1)S(1)} %slice.196), channel_id=1, source_target_pairs={{0,4},{4,8},{8,12},{12,16},{16,20},{20,24},{24,28},{28,32},{32,36}... | collective-permute-start | bytes 282632 | tf_op jit(solution)/shard_map/ppermute | solution.py:11
  161.8 4.3 %copy-start.2 = (bf16[279,2048]{1,0:T(8,128)(2,1)}, bf16[279,2048]{1,0:T(8,128)(2,1)S(1)}, u32[]{:S(2)}) copy-start(bf16[279,2048]{1,0:T(8,128)(2,1)S(1)} %get-tuple-element.4) | copy-start | bytes 3428356
  178.0 9.8 %copy-start.1 = (f32[256,1024]{1,0:T(8,128)}, f32[256,1024]{1,0:T(8,128)S(1)}, u32[]{:S(2)}) copy-start(f32[256,1024]{1,0:T(8,128)S(1)} %fusion.4) | copy-start | bytes 3145732
  178.0 5.8 %copy-start.3 = (bf16[1024]{0:T(1024)(128)(2,1)S(1)}, bf16[1024]{0:T(1024)(128)(2,1)}, u32[]{:S(2)}) copy-start(bf16[1024]{0:T(1024)(128)(2,1)} %param.4) | copy-start | bytes 6148
  179.2 19.7 %all-to-all-start = ((f32[256,4,256]{2,0,1:T(8,128)}), f32[256,4,256]{2,0,1:T(8,128)S(1)}, u32[]{:S(2)}, u32[]{:S(2)}) async-start(f32[256,4,256]{2,0,1:T(8,128)} %bitcast.10), calls=%async_computation | async-start | bytes 2097152 | tf_op jit(solution)/shard_map/all_to_all | solution.py:52
  183.8 4.0 %copy-start = (bf16[1024,2048]{1,0:T(8,128)(2,1)S(1)}, bf16[1024,2048]{1,0:T(8,128)(2,1)}, u32[]{:S(2)}) copy-start(bf16[1024,2048]{1,0:T(8,128)(2,1)} %all-gather.2.cloned.1.call-done) | copy-start | bytes 12582916
  199.2 31.0 %collective-permute-start.3 = (f32[256,1024]{1,0:T(8,128)S(1)}, f32[256,1024]{1,0:T(8,128)S(1)}, u32[]{:S(2)}, u32[]{:S(2)}) collective-permute-start(f32[256,1024]{1,0:T(8,128)S(1)} %bitcast.14), channel_id=1, source_target_pairs={{0,4},{4,8},{8,12},{12,16},{16,20},{20,24},{24,28},{28,32},{32,36}... | collective-permute-start | bytes 3145736 | tf_op jit(solution)/shard_map/ppermute | solution.py:11
Sparse Core Ops, SparseCore 0:
  10.1 51.9 all-gather.1
where the time goes:
time: 239 us; the launch traced here: 238 us
  waiting for transfers between devices  166 us (69%)
  other arithmetic  27.8 us (12%)
  starting transfers between devices  19.6 us (8%)
  between operations  14.8 us (6%)
  matrix products  6.88 us (3%)
  local copies, waits for them, and re-layouts  3.45 us (1%)
    ppermute x4, waiting for transfers between devices, passed_along(): lax.ppermute(shard, axis, [(i, (i + by) % size) for i in range(size)])  103 us
    all_gather x1, waiting for transfers between devices, per_device(): whole = lax.all_gather(series, 'feat', axis=1, tiled=True)  54.2 us
    exp x2, other arithmetic, kernel_tile(): return jnp.exp(-dist / denom)  16.9 us
    ppermute x4, starting transfers between devices, passed_along(): lax.ppermute(shard, axis, [(i, (i + by) % size) for i in range(size)])  15 us
    reduce_sum x2, other arithmetic, kernel_tile(): col_sq = jnp.sum(jnp.square(cols_ext.astype(jnp.float32)), axis=1)  8.26 us
    all_to_all x1, waiting for transfers between devices, per_device(): lax.all_to_all(following, 'feat', split_axis=1, concat_axis=0, tiled=True)  8.09 us
    dot_general x2, matrix products, kernel_tile(): lax.dot_general(rows_ext, cols_ext, (((1,), (1,)), ((), ())), preferred_e...  6.88 us
  transfers between devices with their start and end apart: 6, of which 4 were waited for; matrix products, arithmetic and copies ran while one was open for 8% of the time, Pallas kernels for 0%

commit v1 on v0

v1 whole, which is shorter than its diff:
```python
import functools

import jax
import jax.numpy as jnp
from jax import lax
from jax.experimental import pallas as pl
from jax.experimental.pallas import tpu as pltpu
from jax.sharding import PartitionSpec as P

LAGS = 24
LEAD = 32
LANE = 128
Z_SIZE = 16
PARTS = 4
MESH = pl.DeviceIdType.MESH
CONTRACT_LAST = (((1,), (1,)), ((), ()))


def multiple(value, of):
    return pl.multiple_of(value, of)


def tiles_kernel(
    blocks,
    series_ref,
    inv_ref,
    width_ref,
    same_ref,
    next_ref,
    prev_ref,
    whole,
    rows,
    nrows,
    ninv,
    gram,
    sums,
    norms,
    row_norms,
    row_factor,
    kept,
    turned,
    same_kept,
    local_sem,
    tail_send,
    tail_recv,
    sib_send,
    sib_recv,
    hop,
    turn_hop,
    raw_relay,
    tile_relay,
    hop_send,
    hop_recv,
    far_send,
    far_recv,
    pass_send,
    pass_recv,
    rows_send,
    rows_recv,
    inv_send,
    inv_recv,
    prev_send,
    prev_recv,
    turn_send,
    turn_recv,
    turn_hop_send,
    turn_hop_recv,
    raw_send,
    raw_recv,
    tile_send,
    tile_recv,
):
    block, quarter = series_ref.shape
    dims = 4 * quarter
    share = block // 4
    wide = block + LANE
    past = wide - LEAD

    b, f = lax.axis_index("blk"), lax.axis_index("feat")
    core, chip = lax.rem(f, 2), f // 2
    sib, far, cross = f + 1 - 2 * core, lax.rem(f + 2, 4), 3 - f
    after, before = lax.rem(b + 1, blocks), lax.rem(b + blocks - 1, blocks)
    half = blocks // 2
    pos, first = lax.rem(b, half), (b // half) * half
    over = lax.rem(b + half, blocks)
    near, side_z, side_x, end = first, first + Z_SIZE - 1, first + half - Z_SIZE, first + half - 1
    is_near, is_end = pos == 0, pos == half - 1
    is_side_z, is_side_x = pos == Z_SIZE - 1, pos == half - Z_SIZE
    is_side = jnp.logical_or(is_side_z, is_side_x)
    is_corner = jnp.logical_or(is_side, jnp.logical_or(is_near, is_end))
    others = (sib, far, cross)
    everyone = (f, sib, far, cross)

    barrier = pltpu.get_barrier_semaphore()
    peers = [(b, j) for j in others] + [(n, j) for n in (after, before) for j in everyone]
    peers += [(over, j) for j in (f, far, sib)]
    for peer in peers:
        pl.semaphore_signal(barrier, inc=1, device_id=peer, device_id_type=MESH)

    @pl.when(is_corner)
    def _():
        for corner in (near, side_z, side_x, end):

            @pl.when(corner != b)
            def _():
                pl.semaphore_signal(barrier, inc=1, device_id=(corner, f), device_id_type=MESH)

    @pl.when(is_corner)
    def _():
        pl.semaphore_wait(barrier, len(peers) + 3)

    @pl.when(jnp.logical_not(is_corner))
    def _():
        pl.semaphore_wait(barrier, len(peers))

    sent = []

    def post(src, dst, send_sem, recv_sem, to):
        pltpu.make_async_remote_copy(
            src_ref=src, dst_ref=dst, send_sem=send_sem, recv_sem=recv_sem, device_id=to, device_id_type=MESH
        ).start()

    def leaves(src, send_sem, recv_sem):
        sent.append(
            pltpu.make_async_remote_copy(
                src_ref=src, dst_ref=src, send_sem=send_sem, recv_sem=recv_sem, device_id=(b, sib), device_id_type=MESH
            )
        )

    def send(src, dst, send_sem, recv_sem, to):
        post(src, dst, send_sem, recv_sem, to)
        leaves(src, send_sem, recv_sem)

    def receive(dst, send_sem, recv_sem, sender):
        pltpu.make_async_remote_copy(
            src_ref=dst, dst_ref=dst, send_sem=send_sem, recv_sem=recv_sem, device_id=sender, device_id_type=MESH
        ).wait_recv()

    def cols(q):
        return pl.ds(multiple(q * quarter, quarter), quarter)

    def group(g):
        return pl.ds(multiple(g * share, share), share)

    def chunk(c, k):
        return group(lax.rem(2 * c + k, 4))

    here = pltpu.make_async_copy(series_ref, whole.at[pl.ds(0, block), cols(f)], local_sem.at[0])
    here.start()
    for i, j in enumerate(everyone):
        send(
            series_ref.at[pl.ds(block - LEAD, LEAD), :],
            whole.at[pl.ds(past, LEAD), cols(f)],
            tail_send.at[i],
            tail_recv.at[i],
            (after, j),
        )
    def halved(c, k, s):
        return pl.ds(multiple(lax.rem(2 * c + k, 4) * share + s * (share // 2), share // 2), share // 2)

    def set_out(k):
        for s, j in enumerate((f, far)):
            i = 4 * s + k
            send(
                series_ref.at[halved(1 - chip, k, s), :], hop.at[s, k], hop_send.at[i], hop_recv.at[i], (over, j)
            )

    def hand_over(k):
        for s, j in enumerate((f, far)):
            i = 4 * s + k
            receive(hop.at[s, k], hop_send.at[i], hop_recv.at[i], (over, j))
            c, to = (1 - chip, far) if s == 0 else (chip, f)
            send(hop.at[s, k], whole.at[halved(c, k, s), cols(j)], far_send.at[i], far_recv.at[i], (over, to))

    set_out(0)
    set_out(1)
    send(series_ref, whole.at[pl.ds(0, block), cols(f)], sib_send.at[0], sib_recv.at[0], (b, sib))
    send(inv_ref, ninv, inv_send.at[0], inv_recv.at[0], (before, f))

    def send_rows(q, i, src):
        @pl.when(pos != 0)
        def _():
            post(src, nrows.at[pl.ds(LEAD, share), cols(q)], rows_send.at[i], rows_recv.at[i], (before, f))

        @pl.when(pos == 0)
        def _():
            to = (side_z, side_x, over, end)[i]
            slot = 1 if i == 2 else 0
            post(src, raw_relay.at[slot], rows_send.at[i], raw_recv.at[slot], (to, f))

        leaves(src, rows_send.at[i], rows_recv.at[i])

    def relay_onward(buffer, slot, send_sem, recv_sem, sender, cases):
        receive(buffer.at[slot], send_sem.at[slot], recv_sem.at[slot], sender)
        for here_is, dst, dst_sem, to in cases:

            @pl.when(here_is)
            def _():
                post(buffer.at[slot], dst, send_sem.at[slot], dst_sem, to)

    def row_piece(i):
        return nrows.at[pl.ds(LEAD, share), cols(everyone[i])]

    def raw_out(here_is):
        @pl.when(here_is)
        def _():
            cases = (
                (is_end, row_piece(3), rows_recv.at[3], (over, f)),
                (is_side, raw_relay.at[1], raw_recv.at[1], (over, f)),
            )
            relay_onward(raw_relay, 0, raw_send, raw_recv, (near, f), cases)

    def raw_in(here_is):
        @pl.when(here_is)
        def _():
            cases = (
                (is_near, row_piece(2), rows_recv.at[2], (end, f)),
                (is_side_z, row_piece(0), rows_recv.at[0], (end, f)),
                (is_side_x, row_piece(1), rows_recv.at[1], (end, f)),
            )
            relay_onward(raw_relay, 1, raw_send, raw_recv, (over, f), cases)

    send_rows(f, 0, series_ref.at[group(f), :])
    whole[pl.ds(block, LANE - LEAD), :] = jnp.zeros((LANE - LEAD, dims), whole.dtype)
    gram[pl.ds(0, 8), :] = jnp.zeros((8, wide), jnp.float32)

    receive(whole.at[pl.ds(0, block), cols(sib)], sib_send.at[0], sib_recv.at[0], (b, sib))
    send_rows(sib, 1, whole.at[group(f), cols(sib)])

    def pass_on(k):
        part = chunk(chip, k)
        for s in range(2):
            i = 4 * s + k
            receive(
                whole.at[halved(chip, k, s), cols(far)], far_send.at[i], far_recv.at[i], (over, far if s == 0 else f)
            )
        send(whole.at[part, cols(far)], whole.at[part, cols(far)], pass_send.at[k], pass_recv.at[k], (b, sib))

    def passed(k):
        receive(whole.at[chunk(chip, k), cols(cross)], pass_send.at[k], pass_recv.at[k], (b, sib))

    hand_over(0)
    set_out(2)
    hand_over(1)
    set_out(3)
    pass_on(0)
    raw_out(is_side)
    hand_over(2)
    pass_on(1)
    send_rows(far, 2, whole.at[group(f), cols(far)])
    passed(0)
    passed(1)
    send_rows(cross, 3, whole.at[group(f), cols(cross)])
    raw_in(is_side)
    hand_over(3)
    pass_on(2)
    pass_on(3)
    raw_in(is_near)
    raw_out(is_end)
    passed(2)
    passed(3)
    for i, j in enumerate(everyone):
        receive(whole.at[pl.ds(past, LEAD), cols(j)], tail_send.at[i], tail_recv.at[i], (before, j))
    here.wait()
    lead = multiple(lax.rem(f * share + wide - LEAD, wide), LEAD)
    send(
        whole.at[pl.ds(lead, LEAD), :], nrows.at[pl.ds(0, LEAD), :], rows_send.at[4], rows_recv.at[4], (before, f)
    )

    def squares(x):
        total = jnp.zeros((x.shape[0], LANE), jnp.float32)
        for g in range(dims // LANE):
            piece = x[:, g * LANE : (g + 1) * LANE].astype(jnp.float32)
            total = total + piece * piece
        return total

    def norm_step(j, carry):
        part = pl.ds(multiple(j * LANE, LANE), LANE)
        norms[:, part] = jnp.broadcast_to(jnp.sum(squares(whole[part, :]).T, axis=0, keepdims=True), (8, LANE))
        return carry

    lax.fori_loop(0, wide // LANE, norm_step, 0)

    def lag_sum(x, axis):
        for step in (1, 2, 4):
            x = x + pltpu.roll(x, step, axis)
        return x + pltpu.roll(x, 8, axis) + pltpu.roll(x, 16, axis)

    norms[...] = lag_sum(norms[...], 1)
    inv_row = jnp.concatenate([inv_ref[j : j + 1, :] for j in range(block // LANE)], axis=1)
    width_row = jnp.full((1, LANE), width_ref[0], jnp.float32) * (LAGS * dims)

    def factors(ref):
        for j in range(share // LANE):
            line = ref[pl.ds(f * (share // LANE) + j, 1), :] / width_row
            row_factor[pl.ds(j * LANE, LANE), :] = jnp.broadcast_to(-line, (LANE, LANE)).T

    def tile(source, target, ready):
        def gram_step(j, carry):
            part = pl.ds(multiple(j * 256, 256), 256)
            gram[pl.ds(8, LEAD + share), part] = lax.dot_general(
                source[...], whole[part, :], CONTRACT_LAST, preferred_element_type=jnp.float32
            )
            return carry

        lax.fori_loop(0, block // 256, gram_step, 0)
        gram[pl.ds(8, LEAD + share), pl.ds(block, LANE)] = lax.dot_general(
            source[...], whole[pl.ds(block, LANE), :], CONTRACT_LAST, preferred_element_type=jnp.float32
        )

        def eight_lags(t, carry):
            x = gram[pl.ds(multiple(t * 32, 32), 40), :]
            for step in (1, 2, 4):
                x = x + pltpu.roll(pltpu.roll(x, step, 0), step, 1)
            sums[pl.ds(multiple(t * 32, 32), 32), :] = x[8:, :]
            return carry

        lax.fori_loop(0, (LEAD + share) // 32, eight_lags, 0)

        def finish(t, carry):
            x = sums[pl.ds(multiple(t * 32 + 32, 32), 32), :]
            x = x + pltpu.roll(sums[pl.ds(multiple(t * 32 + 24, 8), 32), :], 8, 1)
            x = x + pltpu.roll(sums[pl.ds(multiple(t * 32 + 16, 8), 32), :], 16, 1)
            part = pl.ds(multiple(t * 32, 32), 32)
            spread = row_norms[part, :][:, :1] + norms[pl.ds(0, 1), pl.ds(0, block)] - 2.0 * x[:, :block]
            target[part, :] = jnp.exp(spread * (row_factor[part, :][:, :1] * inv_row))
            return carry

        per = share // 32 // PARTS
        for h in range(PARTS):
            lax.fori_loop(h * per, (h + 1) * per, finish, 0)
            ready(pl.ds(h * per * 32, per * 32), h)

    for i, j in enumerate(everyone):
        receive(nrows.at[pl.ds(LEAD, share), cols(j)], rows_send.at[i], rows_recv.at[i], (after, f))
    receive(nrows.at[pl.ds(0, LEAD), :], rows_send.at[4], rows_recv.at[4], (after, f))
    receive(ninv, inv_send.at[0], inv_recv.at[0], (after, f))
    factors(ninv)
    lagged = jnp.broadcast_to(jnp.sum(squares(nrows[...]), axis=1, keepdims=True), (LEAD + share, LANE))
    row_norms[...] = lag_sum(lagged, 0)[LEAD:, :]

    def send_prev(part, h):
        @pl.when(pos != half - 1)
        def _():
            post(kept.at[part, :], prev_ref.at[part, :], prev_send.at[h], prev_recv.at[h], (after, f))

        @pl.when(pos == half - 1)
        def _():
            to = (side_z, side_x, near, over)[h]
            slot = 1 if h == 3 else 0
            post(kept.at[part, :], tile_relay.at[slot], prev_send.at[h], tile_recv.at[slot], (to, f))

        leaves(kept.at[part, :], prev_send.at[h], prev_recv.at[h])

    tile(nrows, kept, send_prev)

    def turn_step(j, carry):
        part = pl.ds(multiple(j * LANE, LANE), LANE)
        turned[part, :] = kept[:, part].T
        return carry

    lax.fori_loop(0, block // LANE, turn_step, 0)
    own_columns = pl.ds(multiple(f * share, share), share)
    send(turned.at[group(far), :], turn_hop.at[0], turn_hop_send.at[0], turn_hop_recv.at[0], (over, f))
    send(turned.at[group(cross), :], turn_hop.at[1], turn_hop_send.at[1], turn_hop_recv.at[1], (over, far))
    send(turned.at[group(sib), :], next_ref.at[:, own_columns], turn_send.at[2], turn_recv.at[2], (b, sib))
    own_turned = pltpu.make_async_copy(turned.at[group(f), :], next_ref.at[:, own_columns], local_sem.at[1])
    own_turned.start()

    rows[pl.ds(0, LEAD), :] = whole[pl.ds(lead, LEAD), :]
    rows[pl.ds(LEAD, share), :] = whole[group(f), :]
    factors(inv_ref)
    for j in range(share // LANE):
        line = norms[pl.ds(0, 1), pl.ds(multiple(f * share + j * LANE, LANE), LANE)]
        row_norms[pl.ds(j * LANE, LANE), :] = jnp.broadcast_to(line, (LANE, LANE)).T
    tile(rows, same_kept, lambda part, h: None)
    own_same = pltpu.make_async_copy(same_kept, same_ref, local_sem.at[2])
    own_same.start()

    for s, j, to in ((0, f, far), (1, far, sib)):
        receive(turn_hop.at[s], turn_hop_send.at[s], turn_hop_recv.at[s], (over, j))
        send(turn_hop.at[s], next_ref.at[:, group(j)], turn_send.at[s], turn_recv.at[s], (over, to))

    def piece(h):
        return pl.ds(h * (share // PARTS), share // PARTS)

    def tile_piece(h):
        return prev_ref.at[piece(h), :]

    @pl.when(jnp.logical_or(is_near, is_side))
    def _():
        cases = (
            (is_near, tile_piece(2), prev_recv.at[2], (over, f)),
            (is_side, tile_relay.at[1], tile_recv.at[1], (over, f)),
        )
        relay_onward(tile_relay, 0, tile_send, tile_recv, (end, f), cases)

    @pl.when(jnp.logical_or(is_end, is_side))
    def _():
        cases = (
            (is_end, tile_piece(3), prev_recv.at[3], (near, f)),
            (is_side_z, tile_piece(0), prev_recv.at[0], (near, f)),
            (is_side_x, tile_piece(1), prev_recv.at[1], (near, f)),
        )
        relay_onward(tile_relay, 1, tile_send, tile_recv, (over, f), cases)

    for h in range(PARTS):
        receive(tile_piece(h), prev_send.at[h], prev_recv.at[h], (before, f))
    for i, j in enumerate((far, cross, sib)):
        receive(next_ref.at[:, group(j)], turn_send.at[i], turn_recv.at[i], (b, j))
    own_turned.wait()
    own_same.wait()
    for copy in sent:
        copy.wait_send()

    def relayed(here_is, buffer, slot, send_sem, recv_sem):
        @pl.when(here_is)
        def _():
            pltpu.make_async_remote_copy(
                src_ref=buffer.at[slot],
                dst_ref=buffer.at[slot],
                send_sem=send_sem.at[slot],
                recv_sem=recv_sem.at[slot],
                device_id=(over, f),
                device_id_type=MESH,
            ).wait_send()

    relayed(jnp.logical_or(is_end, is_side), raw_relay, 0, raw_send, raw_recv)
    relayed(jnp.logical_or(is_near, is_side), raw_relay, 1, raw_send, raw_recv)
    relayed(jnp.logical_or(is_near, is_side), tile_relay, 0, tile_send, tile_recv)
    relayed(jnp.logical_or(is_end, is_side), tile_relay, 1, tile_send, tile_recv)


def per_device(blocks, series, scales, width):
    block, quarter = series.shape
    dims, share, wide = 4 * quarter, block // 4, block + LANE
    inv = (1.0 / scales.astype(jnp.float32)).reshape(block // LANE, LANE)
    out = jax.ShapeDtypeStruct((share, block), jnp.float32)
    dma = lambda n: pltpu.SemaphoreType.DMA((n,))
    early = (4, 4, 1, 1)
    late = (8, 8, 8, 8, 4, 4, 5, 5, 1, 1, PARTS, PARTS, 3, 3, 2, 2, 2, 2, 2, 2)
    return pl.pallas_call(
        functools.partial(tiles_kernel, blocks),
        out_shape=(out, out, out),
        in_specs=[
            pl.BlockSpec(memory_space=pl.ANY),
            pl.BlockSpec(memory_space=pltpu.VMEM),
            pl.BlockSpec(memory_space=pltpu.SMEM),
        ],
        out_specs=(pl.BlockSpec(memory_space=pl.ANY),) * 3,
        scratch_shapes=[
            pltpu.VMEM((wide, dims), series.dtype),
            pltpu.VMEM((LEAD + share, dims), series.dtype),
            pltpu.VMEM((LEAD + share, dims), series.dtype),
            pltpu.VMEM((block // LANE, LANE), jnp.float32),
            pltpu.VMEM((8 + LEAD + share, wide), jnp.float32),
            pltpu.VMEM((LEAD + share, wide), jnp.float32),
            pltpu.VMEM((8, wide), jnp.float32),
            pltpu.VMEM((share, LANE), jnp.float32),
            pltpu.VMEM((share, LANE), jnp.float32),
            pltpu.VMEM((share, block), jnp.float32),
            pltpu.VMEM((block, share), jnp.float32),
            pltpu.VMEM((share, block), jnp.float32),
            dma(3),
        ]
        + [dma(n) for n in early]
        + [
            pltpu.VMEM((2, 4, share // 2, quarter), series.dtype),
            pltpu.VMEM((2, share, share), jnp.float32),
            pltpu.VMEM((2, share, quarter), series.dtype),
            pltpu.VMEM((2, share // PARTS, block), jnp.float32),
        ]
        + [dma(n) for n in late],
        compiler_params=pltpu.CompilerParams(
            collective_id=0, has_side_effects=True, vmem_limit_bytes=48 * 1024 * 1024
        ),
    )(series, inv, width)


def solution(mesh):
    in_specs = (P("blk", "feat"), P("blk"), P())
    out_specs = (P(("blk", "feat"), None), P(("blk", "feat"), None), P(("blk", "feat"), None))
    return jax.shard_map(
        functools.partial(per_device, mesh.shape["blk"]),
        mesh=mesh,
        in_specs=in_specs,
        out_specs=out_specs,
        check_vma=False,
    )
```

time: 239 us -> 98.5 us (0.41)
  waiting for transfers between devices: 166 us -> 0 us
  Pallas kernels: 0 us -> 92.2 us
  other arithmetic: 27.8 us -> 0.69 us
  starting transfers between devices: 19.6 us -> 0 us
  between operations: 14.8 us -> 1.29 us
  matrix products: 6.88 us -> 0 us
    ppermute x4 -> x0, waiting for transfers between devices: 103 us -> none  [passed_along(): lax.ppermute(shard, axis, [(i, (i + by) % size) for i in range(size)])]
    pallas_call x0 -> x1, Pallas kernels: none -> 92.2 us  [per_device(): pl.pallas_call(functools.partial(tiles_kernel, blocks), out_shape=(out, o...]
    all_gather x1 -> x0, waiting for transfers between devices: 54.2 us -> none  [per_device(): whole = lax.all_gather(series, 'feat', axis=1, tiled=True)]
    exp x2 -> x0, other arithmetic: 16.9 us -> none  [kernel_tile(): return jnp.exp(-dist / denom)]
    ppermute x4 -> x0, starting transfers between devices: 15 us -> none  [passed_along(): lax.ppermute(shard, axis, [(i, (i + by) % size) for i in range(size)])]
    reduce_sum x3 -> x0, other arithmetic: 10.1 us -> none  [the longest x2 8.26 us: kernel_tile(): col_sq = jnp.sum(jnp.square(cols_ext.astype(jnp.float32)), axis=1)]
    all_to_all x1 -> x0, waiting for transfers between devices: 8.09 us -> none  [per_device(): lax.all_to_all(following, 'feat', split_axis=1, concat_axis=0, tiled=True)]
    dot_general x2 -> x0, matrix products: 6.88 us -> none  [kernel_tile(): lax.dot_general(rows_ext, cols_ext, (((1,), (1,)), ((), ())), preferred_e...]
  transfers between devices with their start and end apart: 6 -> 0, of which waited for: 4 -> 0; matrix products, arithmetic and copies ran while one was open for 8% -> 0% of each run, Pallas kernels for 0% -> 0%
where the time goes in v1:
time: 98.5 us; the launch traced here: 98.3 us
  Pallas kernels  92.2 us (94%)
  local copies, waits for them, and re-layouts  4.14 us (4%)
  between operations  1.29 us (1%)
    pallas_call x1, Pallas kernels, per_device(): pl.pallas_call(functools.partial(tiles_kernel, blocks), out_shape=(out, o...  92.2 us
    unnamed x5, local copies, waits for them, and re-layouts  4.14 us

profile of v1, /device:TPU:1, one launch (start us, length us, event | category | flops | bytes accessed | tf_op | source)
XLA Modules:
  0.0 98.3 jit_solution(537493654041617837)
XLA Ops:
  1.3 0.7 divide_bitcast_fusion.inv_ref
  2.0 0.0 copy-start
  2.0 1.2 %copy-done = bf16[1024,512]{1,0:T(8,128)(2,1)S(1)} copy-done((bf16[1024,512]{1,0:T(8,128)(2,1)S(1)}, bf16[1024,512]{1,0:T(8,128)(2,1)}, u32[]{:S(2)}) %copy-start) | copy-done | bytes 1048600
  3.2 92.2 %shard_map.58 = (f32[256,1024]{1,0:T(8,128)S(1)}, f32[256,1024]{1,0:T(8,128)S(1)}, f32[256,1024]{1,0:T(8,128)S(1)}) custom-call(bf16[1024,512]{1,0:T(8,128)(2,1)S(1)} %copy-done, f32[8,128]{1,0:T(8,128)S(1)} %divide_bitcast_fusion.inv_ref, f32[1]{0:T(128)S(6)} %copy.9.width_ref), custom_call_target="tpu_custom_call" | custom-call | tf_op jit(solution)/shard_map/pallas_call | solution.py:442
  95.4 1.0 copy.10
  96.4 1.0 copy.11
  97.3 1.0 copy.12
Async XLA Ops:
  2.0 1.2 %copy-start = (bf16[1024,512]{1,0:T(8,128)(2,1)S(1)}, bf16[1024,512]{1,0:T(8,128)(2,1)}, u32[]{:S(2)}) copy-start(bf16[1024,512]{1,0:T(8,128)(2,1)} %series_ref.1) | copy-start | bytes 3145732

commit v2 on v0

v2 whole, which is shorter than its diff:
```python
import functools

import jax
import jax.numpy as jnp
from jax import lax
from jax.experimental import pallas as pl
from jax.experimental.pallas import tpu as pltpu
from jax.sharding import PartitionSpec as P

LAGS = 24
LEAD = 32
LANE = 128
Z_SIZE = 16
CHUNKS = 8
PIECES = 8
MESH = pl.DeviceIdType.MESH
CONTRACT_LAST = (((1,), (1,)), ((), ()))


def multiple(value, of):
    return pl.multiple_of(value, of)


def tiles_kernel(
    blocks,
    series_ref,
    inv_ref,
    width_ref,
    same_ref,
    next_ref,
    prev_ref,
    whole,
    rows,
    nrows,
    mrows,
    ninv,
    minv,
    gram,
    mgram,
    same_gram,
    sums,
    norms,
    row_norms,
    row_factor,
    kept,
    mkept,
    turned,
    mturned,
    same_kept,
    hop,
    turn_hop,
    mturn_hop,
    k_relay,
    mk_relay,
    local_sem,
    tail_send,
    tail_recv,
    sib_send,
    sib_recv,
    hop_send,
    hop_recv,
    far_send,
    far_recv,
    pass_send,
    pass_recv,
    lead_send,
    lead_recv,
    inv_send,
    inv_recv,
    turn_send,
    turn_recv,
    turn_hop_send,
    turn_hop_recv,
    n_send,
    n_recv,
    m_send,
    m_recv,
    k_send,
    k_recv,
    mk_send,
    mk_recv,
    ride_send,
    relay_send,
    relay_recv,
):
    block, quarter = series_ref.shape
    dims = 4 * quarter
    share = block // 4
    part_rows = share // 2
    wide = block + LANE
    past = wide - LEAD

    b, f = lax.axis_index("blk"), lax.axis_index("feat")
    core, chip = lax.rem(f, 2), f // 2
    sib, far, cross = f + 1 - 2 * core, lax.rem(f + 2, 4), 3 - f
    after, before = lax.rem(b + 1, blocks), lax.rem(b + blocks - 1, blocks)
    half = blocks // 2
    pos, first = lax.rem(b, half), (b // half) * half
    over = lax.rem(b + half, blocks)
    others = (sib, far, cross)
    everyone = (f, sib, far, cross)
    near, end = first, first + half - 1
    side_pos = (Z_SIZE - 1, half - Z_SIZE, Z_SIZE, half - Z_SIZE - 1, 2 * Z_SIZE, 2 * Z_SIZE - 1)
    is_near, is_end = pos == 0, pos == half - 1
    is_sides = [pos == p for p in side_pos]
    any_of = lambda conditions: functools.reduce(jnp.logical_or, conditions)
    is_side = any_of(is_sides)
    is_seam = jnp.logical_or(is_near, is_end)
    ordinary = jnp.logical_not(is_seam)

    barrier = pltpu.get_barrier_semaphore()
    peers = [(b, j) for j in others] + [(after, f), (before, f)] + [(over, j) for j in (f, far, sib)]
    for peer in peers:
        pl.semaphore_signal(barrier, inc=1, device_id=peer, device_id_type=MESH)

    def greet(condition, corners):
        @pl.when(condition)
        def _():
            for corner in corners:
                pl.semaphore_signal(barrier, inc=1, device_id=corner, device_id_type=MESH)
            pl.semaphore_wait(barrier, len(peers) + len(corners))

    sides = [first + p for p in side_pos]
    greet(is_near, [(side, f) for side in sides] + [(end, f), (end, sib)])
    greet(is_end, [(side, f) for side in sides] + [(near, f), (near, sib)])
    greet(is_side, [(near, f), (end, f)])

    @pl.when(jnp.logical_not(jnp.logical_or(is_seam, is_side)))
    def _():
        pl.semaphore_wait(barrier, len(peers))

    sent = []

    def copy_of(src, dst, send_sem, recv_sem, to):
        return pltpu.make_async_remote_copy(
            src_ref=src, dst_ref=dst, send_sem=send_sem, recv_sem=recv_sem, device_id=to, device_id_type=MESH
        )

    def post(src, dst, send_sem, recv_sem, to):
        copy_of(src, dst, send_sem, recv_sem, to).start()

    def leaves(src, send_sem, recv_sem, condition=None):
        sent.append((condition, copy_of(src, src, send_sem, recv_sem, (b, sib))))

    def send(src, dst, send_sem, recv_sem, to):
        post(src, dst, send_sem, recv_sem, to)
        leaves(src, send_sem, recv_sem)

    def receive(dst, send_sem, recv_sem, sender):
        copy_of(dst, dst, send_sem, recv_sem, sender).wait_recv()

    def when(condition, act):
        @pl.when(condition)
        def _():
            act()

    def cols(q):
        return pl.ds(multiple(q * quarter, quarter), quarter)

    def group(g):
        return pl.ds(multiple(g * share, share), share)

    class Route:
        def __init__(self, back, spot, relay, i, send_sem, recv_sem):
            self.back, self.spot, self.relay, self.i = back, spot, relay, i
            self.send_sem, self.recv_sem = send_sem, recv_sem
            self.to, self.sender = (before, after) if back else (after, before)
            self.is_origin, self.origin, self.goal = (is_near, near, end) if back else (is_end, end, near)

        def slot(self, s):
            return self.relay.at[s], relay_send.at[2 * self.i + s], relay_recv.at[2 * self.i + s]

        def start(self, p, src):
            def direct():
                post(src, self.spot(p), self.send_sem.at[p], self.recv_sem.at[p], (self.to, f))

            def detour():
                if p < 6:
                    by, s = sides[p], 0
                elif p == 6:
                    by, s = (over, 1) if self.back else (near, 0)
                else:
                    by, s = (end, 0) if self.back else (over, 1)
                buffer, _, recv_sem = self.slot(s)
                post(src, buffer, self.send_sem.at[p], recv_sem, (by, f))

            when(self.is_origin, detour)
            when(jnp.logical_not(self.is_origin), direct)

        def register(self, p, src):
            leaves(src, self.send_sem.at[p], self.recv_sem.at[p])

        def go(self, p, src):
            self.start(p, src)
            self.register(p, src)

        def await_piece(self, p):
            receive(self.spot(p), self.send_sem.at[p], self.recv_sem.at[p], (self.sender, f))

        def forward(self, condition, s, sender, dst, dst_sem, to):
            def act():
                buffer, send_sem, recv_sem = self.slot(s)
                receive(buffer, send_sem, recv_sem, (sender, f))
                post(buffer, dst, send_sem, dst_sem, (to, f))

            when(condition, act)

        def outward(self, condition):
            buffer, _, recv_sem = self.slot(1)
            self.forward(condition, 0, self.origin, buffer, recv_sem, over)

        def inward(self, condition):
            for p in range(6):
                self.forward(
                    jnp.logical_and(condition, is_sides[p]), 1, over, self.spot(p), self.recv_sem.at[p], self.goal
                )

        def at_seam(self):
            p, q = (7, 6) if self.back else (6, 7)
            at_p, at_q = (is_end, is_near) if self.back else (is_near, is_end)
            self.forward(at_p, 0, self.origin, self.spot(p), self.recv_sem.at[p], over)
            self.forward(at_q, 1, over, self.spot(q), self.recv_sem.at[q], self.goal)

        def drain(self):
            at_p, at_q = (is_end, is_near) if self.back else (is_near, is_end)
            for s, condition in ((0, at_p), (1, at_q)):
                buffer, send_sem, recv_sem = self.slot(s)
                copy = copy_of(buffer, buffer, send_sem, recv_sem, (over, f))
                when(jnp.logical_or(is_side, condition), copy.wait_send)

    def n_spot(p):
        return nrows.at[pl.ds(LEAD + (p % 2) * part_rows, part_rows), cols(everyone[p // 2])]

    def m_spot(p):
        size = part_rows // 2
        return mrows.at[pl.ds(LEAD + (p % 2) * size, size), cols(everyone[p // 2])]

    def k_spot(p):
        g, h = p % 4, p // 4
        return prev_ref.at[pl.ds(h * part_rows, part_rows), pl.ds(g * share + part_rows, part_rows)]

    def mk_spot(p):
        size = part_rows // PIECES
        return next_ref.at[pl.ds(p * size, size), :]

    k_route = Route(False, k_spot, k_relay, 0, k_send, k_recv)
    mk_route = Route(True, mk_spot, mk_relay, 1, mk_send, mk_recv)

    quarter_rows = share // 4

    def own_rows(ref, start, size, columns):
        return ref.at[pl.ds(multiple(f * share + start, size), size), columns]

    def send_n(ref, qi, columns, condition):
        for p in (2 * qi, 2 * qi + 1):
            piece = own_rows(ref, (p % 2) * part_rows, part_rows, columns)
            when(condition, functools.partial(post, piece, n_spot(p), n_send.at[p], n_recv.at[p], (before, f)))

    def send_n_quarter(qi, i, condition):
        p, columns = 2 * qi + i // 2, cols(everyone[qi])
        piece = own_rows(whole, i * quarter_rows, quarter_rows, columns)
        spot = nrows.at[pl.ds(LEAD + i * quarter_rows, quarter_rows), columns]
        when(condition, functools.partial(post, piece, spot, n_send.at[p], n_recv.at[p], (before, f)))

    def send_m(ref, qi, columns, condition, pieces=(0, 1)):
        for i in pieces:
            p = 2 * qi + i
            piece = own_rows(ref, i * quarter_rows, quarter_rows, columns)
            when(condition, functools.partial(post, piece, m_spot(p), m_send.at[p], m_recv.at[p], (after, f)))

    def await_n(p):
        receive(n_spot(p), n_send.at[p], n_recv.at[p], (after, f))

    def await_m(p):
        receive(m_spot(p), m_send.at[p], m_recv.at[p], (before, f))

    has_n, has_m = jnp.logical_not(is_near), jnp.logical_not(is_end)

    def order(c, j):
        return j + c * (2, 2, -1, -3)[j]

    def halved(sender, k, s):
        c = sender if s == 0 else 1 - sender
        usual = order(1 - sender, k // 2) * share + (k % 2) * 2 * quarter_rows + s * quarter_rows
        at_seam = (2 * c + k % 2) * share + (k // 2) * quarter_rows
        return pl.ds(multiple(jnp.where(is_seam, at_seam, usual), quarter_rows), quarter_rows)

    here = pltpu.make_async_copy(series_ref, whole.at[pl.ds(0, block), cols(f)], local_sem.at[0])
    here.start()
    send(
        series_ref.at[pl.ds(block - LEAD, LEAD), :],
        whole.at[pl.ds(past, LEAD), cols(f)],
        tail_send.at[0],
        tail_recv.at[0],
        (after, f),
    )

    def set_out(k):
        for s, j in enumerate((f, far)):
            i = CHUNKS * s + k
            send(series_ref.at[halved(chip, k, s), :], hop.at[s, k], hop_send.at[i], hop_recv.at[i], (over, j))

    def hand_over(k):
        for s, j in enumerate((f, far)):
            i = CHUNKS * s + k
            receive(hop.at[s, k], hop_send.at[i], hop_recv.at[i], (over, j))
            c, to = (chip, far) if s == 0 else (1 - chip, f)
            send(hop.at[s, k], whole.at[halved(c, k, s), cols(j)], far_send.at[i], far_recv.at[i], (over, to))

            to, place = 2 * chip + k % 2, k // 2
            qi = lax.rem(core + k % 2, 2) + 2 * s
            spot = pl.ds(LEAD + place * quarter_rows, quarter_rows)

            def ride_back():
                post(
                    hop.at[s, k], nrows.at[spot, cols(j)], ride_send.at[i], n_recv.at[2 * qi + place // 2], (end, to)
                )

            def ride_on():
                post(hop.at[s, k], mrows.at[spot, cols(j)], ride_send.at[i], m_recv.at[2 * qi + place], (near, to))

            when(is_near, ride_back)
            leaves(hop.at[s, k], ride_send.at[i], n_recv.at[0], is_near)
            if place < 2:
                when(is_end, ride_on)
                leaves(hop.at[s, k], ride_send.at[i], n_recv.at[0], is_end)

    set_out(0)
    set_out(1)
    send(series_ref, whole.at[pl.ds(0, block), cols(f)], sib_send.at[0], sib_recv.at[0], (b, sib))
    send_n(series_ref, 0, slice(None), has_n)
    send_m(series_ref, 0, slice(None), has_m)
    send(inv_ref, ninv, inv_send.at[0], inv_recv.at[0], (before, f))
    send(inv_ref, minv, inv_send.at[1], inv_recv.at[1], (after, f))

    whole[pl.ds(block, LANE - LEAD), :] = jnp.zeros((LANE - LEAD, dims), whole.dtype)
    for buffer in (gram, mgram, same_gram):
        buffer[pl.ds(0, 8), :] = jnp.zeros((8, wide), jnp.float32)

    def pass_on(k):
        for s in range(2):
            i = CHUNKS * s + k
            piece = whole.at[halved(1 - chip, k, s), cols(far)]
            receive(piece, far_send.at[i], far_recv.at[i], (over, far if s == 0 else f))
            send(piece, piece, pass_send.at[i], pass_recv.at[i], (b, sib))

    def passed(k):
        for s in range(2):
            i = CHUNKS * s + k
            piece = whole.at[halved(1 - chip, k, s), cols(cross)]
            receive(piece, pass_send.at[i], pass_recv.at[i], (b, sib))

    lead = multiple(lax.rem(f * share + wide - LEAD, wide), LEAD)
    near_half = pl.ds(multiple(chip * 2 * quarter, quarter), 2 * quarter)
    far_half = pl.ds(multiple((1 - chip) * 2 * quarter, quarter), 2 * quarter)
    leads = (near_half, far_half)
    lead_ways = ((nrows, before, after), (mrows, after, before))

    def post_lead(i):
        for w, (dst, to, _) in enumerate(lead_ways):
            s = 2 * w + i
            post(
                whole.at[pl.ds(lead, LEAD), leads[i]],
                dst.at[pl.ds(0, LEAD), leads[i]],
                lead_send.at[s],
                lead_recv.at[s],
                (to, f),
            )

    def receive_lead(w, i):
        dst, _, sender = lead_ways[w]
        receive(dst.at[pl.ds(0, LEAD), leads[i]], lead_send.at[2 * w + i], lead_recv.at[2 * w + i], (sender, f))

    def squares(x):
        total = jnp.zeros((x.shape[0], LANE), jnp.float32)
        for g in range(x.shape[1] // LANE):
            piece = x[:, g * LANE : (g + 1) * LANE].astype(jnp.float32)
            total = total + piece * piece
        return total

    def norm_of(start):
        part = pl.ds(multiple(start, LANE), LANE)
        norms[:, part] = jnp.broadcast_to(jnp.sum(squares(whole[part, :]).T, axis=0, keepdims=True), (8, LANE))

    def norm_of_group(j):
        for i in range(share // LANE):
            norm_of(order(chip, j) * share + i * LANE)

    def lag_sum(x, axis):
        for step in (1, 2, 4):
            x = x + pltpu.roll(x, step, axis)
        return x + pltpu.roll(x, 8, axis) + pltpu.roll(x, 16, axis)

    def products(left, right):
        return lax.dot_general(left, right, CONTRACT_LAST, preferred_element_type=jnp.float32)

    def same_products(start, size):
        part = pl.ds(multiple(start, LANE), size)
        same_gram[pl.ds(8, LEAD + share), part] = products(rows[...], whole[part, :])

    def add_products(target, source, which, fresh):
        size, height = 256, source.shape[0]
        for start in range(0, wide, size):
            part = pl.ds(start, min(size, wide - start))
            found = products(source[:, which], whole[part, which])
            if fresh:
                target[pl.ds(8, height), part] = found
            else:
                target[pl.ds(8, height), part] += found

    def near_products():
        for p in range(4):
            await_n(p)
        receive_lead(0, 0)
        add_products(gram, nrows, near_half, True)

    both = jnp.logical_and
    first_core, second_core = both(ordinary, core == 0), both(ordinary, core == 1)
    for k in range(CHUNKS):
        hand_over(k)
        if k + 2 < CHUNKS:
            set_out(k + 2)
        if k == 0:
            receive(whole.at[pl.ds(0, block), cols(sib)], sib_send.at[0], sib_recv.at[0], (b, sib))
            send_n(whole, 1, cols(sib), has_n)
            send_m(whole, 1, cols(sib), has_m)
            tail = whole.at[pl.ds(past, LEAD), cols(f)]
            receive(tail, tail_send.at[0], tail_recv.at[0], (before, f))
            for i, j in enumerate(others):
                send(tail, tail, tail_send.at[1 + i], tail_recv.at[1 + i], (b, j))
        else:
            pass_on(k - 1)
        if k == 2:
            here.wait()
            for i, j in enumerate(others):
                receive(whole.at[pl.ds(past, LEAD), cols(j)], tail_send.at[1 + i], tail_recv.at[1 + i], (b, j))
            post_lead(0)
            send_n(whole, 2, cols(far), first_core)
            send_m(whole, 2, cols(far), first_core)
            send_n_quarter(2, 0, is_end)
            send_m(whole, 2, cols(far), is_near, (0,))
        if k == 3:
            send_m(whole, 2, cols(far), second_core)
            passed(0)
            passed(1)
            send_n(whole, 3, cols(cross), first_core)
            send_m(whole, 3, cols(cross), first_core)
            send_n_quarter(3, 0, is_end)
            send_m(whole, 3, cols(cross), is_near, (0,))
            when(ordinary, lambda: norm_of_group(0))
            norm_of(block)
        if k == 4:
            send_n(whole, 2, cols(far), second_core)
            passed(2)
            send_m(whole, 3, cols(cross), second_core)
            send_n_quarter(2, 1, is_end)
            send_m(whole, 2, cols(far), is_near, (1,))
        if k == 5:
            passed(3)
            send_n(whole, 3, cols(cross), second_core)
            send_n_quarter(3, 1, is_end)
            send_m(whole, 3, cols(cross), is_near, (1,))
            when(ordinary, lambda: norm_of_group(1))
        if k == 6:
            send_n_quarter(2, 2, is_end)
            for p in range(4):
                await_m(p)
            receive_lead(1, 0)
            add_products(mgram, mrows, near_half, True)
        if k == 7:
            passed(4)
            passed(5)
            send_n_quarter(3, 2, is_end)
            when(ordinary, lambda: post_lead(1))
            when(ordinary, lambda: norm_of_group(2))
            when(jnp.logical_not(is_end), near_products)
    pass_on(7)
    send_n_quarter(2, 3, is_end)
    passed(6)
    passed(7)
    send_n_quarter(3, 3, is_end)
    when(is_seam, lambda: post_lead(1))
    for i in range(2):
        for w in range(2):
            leaves(whole.at[pl.ds(lead, LEAD), leads[i]], lead_send.at[2 * w + i], lead_recv.at[2 * w + i])
    for p in range(8):
        leaves(n_spot(p), n_send.at[p], n_recv.at[p], has_n)
        leaves(m_spot(p), m_send.at[p], m_recv.at[p], has_m)
    when(ordinary, lambda: norm_of_group(3))

    def all_norms():
        def step(j, carry):
            norm_of(j * LANE)
            return carry

        lax.fori_loop(0, block // LANE, step, 0)

    when(is_seam, all_norms)
    when(is_end, near_products)
    norms[...] = lag_sum(norms[...], 1)

    inv_row = jnp.concatenate([inv_ref[j : j + 1, :] for j in range(block // LANE)], axis=1)
    width_row = jnp.full((1, LANE), width_ref[0], jnp.float32) * (LAGS * dims)

    def factors(ref, count):
        for j in range(count // LANE):
            line = ref[pl.ds(f * (share // LANE) + j, 1), :] / width_row
            row_factor[pl.ds(j * LANE, LANE), :] = jnp.broadcast_to(-line, (LANE, LANE)).T

    def group_norms(near_squares, source):
        height = source.shape[0]
        lagged = jnp.sum(near_squares + squares(source[:, far_half]), axis=1, keepdims=True)
        row_norms[pl.ds(0, height - LEAD), :] = lag_sum(jnp.broadcast_to(lagged, (height, LANE)), 0)[LEAD:, :]

    def all_columns(x):
        return x[:, :block]

    def second_halves(x):
        return jnp.concatenate([x[:, g * share + part_rows : (g + 1) * share] for g in range(4)], axis=1)

    def tile(products_of, target, pick, parts, ready):
        per = target.shape[0] // 32 // parts
        for h in range(parts):
            for t in range(h * per + 1 if h else 0, (h + 1) * per + 1):
                x = products_of[pl.ds(t * 32, 40), :]
                for step in (1, 2, 4):
                    x = x + pltpu.roll(pltpu.roll(x, step, 0), step, 1)
                sums[pl.ds(t * 32, 32), :] = x[8:, :]
            for t in range(h * per, (h + 1) * per):
                x = sums[pl.ds(t * 32 + 32, 32), :]
                x = x + pltpu.roll(sums[pl.ds(t * 32 + 24, 32), :], 8, 1)
                x = x + pltpu.roll(sums[pl.ds(t * 32 + 16, 32), :], 16, 1)
                part = pl.ds(t * 32, 32)
                spread = row_norms[part, :][:, :1] + pick(norms[pl.ds(0, 1), :]) - 2.0 * pick(x)
                target[part, :] = jnp.exp(spread * (row_factor[part, :][:, :1] * pick(inv_row)))
            ready(h)

    receive(minv, inv_send.at[1], inv_recv.at[1], (before, f))
    receive(ninv, inv_send.at[0], inv_recv.at[0], (after, f))
    factors(minv, part_rows)
    m_squares = squares(mrows[:, near_half])
    for p in range(4, 8):
        await_m(p)
    receive_lead(1, 1)
    add_products(mgram, mrows, far_half, False)
    group_norms(m_squares, mrows)

    def send_mk(h):
        for p in range(h * PIECES // 2, (h + 1) * PIECES // 2):
            mk_route.go(p, mkept.at[pl.ds(p * (part_rows // PIECES), part_rows // PIECES), :])

    tile(mgram, mkept, all_columns, 2, send_mk)

    my_columns = pl.ds(multiple(f * share, share), share)
    my_first = pl.ds(multiple(f * share, part_rows), part_rows)
    lower = pl.ds(part_rows, part_rows)
    hops = ((0, far, f), (1, cross, far))

    def turn_m(j):
        for i in range(share // LANE):
            part = pl.ds(multiple(j * share + i * LANE, LANE), LANE)
            mturned[part, :] = mkept[:, part].T

    for s, j, by in hops:
        turn_m(j)
        send(mturned.at[group(j), :], mturn_hop.at[s], turn_hop_send.at[2 + s], turn_hop_recv.at[2 + s], (over, by))
    turn_m(sib)
    send(mturned.at[group(sib), :], prev_ref.at[:, my_first], turn_send.at[5], turn_recv.at[5], (b, sib))
    turn_m(f)
    own_mturned = pltpu.make_async_copy(mturned.at[group(f), :], prev_ref.at[:, my_first], local_sem.at[3])
    own_mturned.start()

    factors(ninv, share)
    n_squares = squares(nrows[:, near_half])
    for p in range(4, 8):
        await_n(p)
    receive_lead(0, 1)
    add_products(gram, nrows, far_half, False)
    group_norms(n_squares, nrows)

    def send_k(h):
        for g in range(4):
            k_route.go(4 * h + g, kept.at[pl.ds(h * part_rows, part_rows), pl.ds(g * part_rows, part_rows)])

    tile(gram, kept, second_halves, 2, send_k)

    def seconds(j):
        return pl.ds(multiple(j * part_rows, part_rows), part_rows)

    def turn(j):
        turned[seconds(j), :] = kept[:, seconds(j)].T

    for s, j, by in hops:
        turn(j)
        send(turned.at[seconds(j), :], turn_hop.at[s], turn_hop_send.at[s], turn_hop_recv.at[s], (over, by))
    turn(sib)
    send(turned.at[seconds(sib), :], next_ref.at[lower, my_columns], turn_send.at[2], turn_recv.at[2], (b, sib))
    turn(f)
    own_turned = pltpu.make_async_copy(turned.at[seconds(f), :], next_ref.at[lower, my_columns], local_sem.at[1])
    own_turned.start()

    def firsts_of(j):
        return pl.ds(multiple(j * share, part_rows), part_rows)

    for s, j, to in ((0, f, far), (1, far, sib)):
        receive(mturn_hop.at[s], turn_hop_send.at[2 + s], turn_hop_recv.at[2 + s], (over, j))
        send(mturn_hop.at[s], prev_ref.at[:, firsts_of(j)], turn_send.at[3 + s], turn_recv.at[3 + s], (over, to))

    rows[pl.ds(0, LEAD), :] = whole[pl.ds(lead, LEAD), :]
    rows[pl.ds(LEAD, share), :] = whole[group(f), :]
    for j in range(4):
        same_products(order(chip, j) * share, share)
    same_products(block, LANE)
    factors(inv_ref, share)
    for j in range(share // LANE):
        line = norms[pl.ds(0, 1), pl.ds(multiple(f * share + j * LANE, LANE), LANE)]
        row_norms[pl.ds(j * LANE, LANE), :] = jnp.broadcast_to(line, (LANE, LANE)).T

    def between(h):
        if h == 0:
            for s, j, to in ((0, f, far), (1, far, sib)):
                receive(turn_hop.at[s], turn_hop_send.at[s], turn_hop_recv.at[s], (over, j))
                send(turn_hop.at[s], next_ref.at[lower, group(j)], turn_send.at[s], turn_recv.at[s], (over, to))
            mk_route.outward(is_side)

    tile(same_gram, same_kept, all_columns, 2, between)
    own_same = pltpu.make_async_copy(same_kept, same_ref, local_sem.at[2])
    own_same.start()

    k_route.outward(is_side)
    mk_route.inward(is_side)
    mk_route.at_seam()
    k_route.inward(is_side)
    k_route.at_seam()

    for p in range(PIECES):
        mk_route.await_piece(p)
        k_route.await_piece(p)
    for i, j in enumerate((far, cross, sib)):
        receive(next_ref.at[lower, group(j)], turn_send.at[i], turn_recv.at[i], (b, j))
        receive(prev_ref.at[:, firsts_of(j)], turn_send.at[3 + i], turn_recv.at[3 + i], (b, j))
    own_turned.wait()
    own_mturned.wait()
    own_same.wait()
    for condition, copy in sent:
        if condition is None:
            copy.wait_send()
        else:
            when(condition, copy.wait_send)
    for route in (k_route, mk_route):
        route.drain()


def per_device(blocks, series, scales, width):
    block, quarter = series.shape
    dims, share, wide = 4 * quarter, block // 4, block + LANE
    part_rows = share // 2
    inv = (1.0 / scales.astype(jnp.float32)).reshape(block // LANE, LANE)
    out = jax.ShapeDtypeStruct((share, block), jnp.float32)
    raw = lambda *shape: pltpu.VMEM(shape, series.dtype)
    wider = lambda *shape: pltpu.VMEM(shape, jnp.float32)
    hops = 2 * CHUNKS
    pairs = (4, 1, hops, hops, hops, 4, 2, 6, 4, PIECES, PIECES, PIECES, PIECES)
    counts = [n for n in pairs for _ in range(2)] + [hops, 4, 4]
    return pl.pallas_call(
        functools.partial(tiles_kernel, blocks),
        out_shape=(out, out, out),
        in_specs=[
            pl.BlockSpec(memory_space=pl.ANY),
            pl.BlockSpec(memory_space=pltpu.VMEM),
            pl.BlockSpec(memory_space=pltpu.SMEM),
        ],
        out_specs=(pl.BlockSpec(memory_space=pl.ANY),) * 3,
        scratch_shapes=[
            raw(wide, dims),
            raw(LEAD + share, dims),
            raw(LEAD + share, dims),
            raw(LEAD + part_rows, dims),
            wider(block // LANE, LANE),
            wider(block // LANE, LANE),
            wider(8 + LEAD + share, wide),
            wider(8 + LEAD + part_rows, wide),
            wider(8 + LEAD + share, wide),
            wider(LEAD + share, wide),
            wider(8, wide),
            wider(share, LANE),
            wider(share, LANE),
            wider(share, block // 2),
            wider(part_rows, block),
            wider(block // 2, share),
            wider(block, part_rows),
            wider(share, block),
            raw(2, CHUNKS, 2 * share // CHUNKS, quarter),
            wider(2, part_rows, share),
            wider(2, share, part_rows),
            wider(2, part_rows, part_rows),
            wider(2, part_rows // PIECES, block),
            pltpu.SemaphoreType.DMA((4,)),
        ]
        + [pltpu.SemaphoreType.DMA((n,)) for n in counts],
        compiler_params=pltpu.CompilerParams(
            collective_id=0, has_side_effects=True, vmem_limit_bytes=48 * 1024 * 1024
        ),
    )(series, inv, width)


def solution(mesh):
    in_specs = (P("blk", "feat"), P("blk"), P())
    out_specs = (P(("blk", "feat"), None), P(("blk", "feat"), None), P(("blk", "feat"), None))
    return jax.shard_map(
        functools.partial(per_device, mesh.shape["blk"]),
        mesh=mesh,
        in_specs=in_specs,
        out_specs=out_specs,
        check_vma=False,
    )
```

time: 239 us -> 81.1 us (0.34)
  waiting for transfers between devices: 166 us -> 0 us
  Pallas kernels: 0 us -> 74.8 us
  other arithmetic: 27.8 us -> 0.69 us
  starting transfers between devices: 19.6 us -> 0 us
  between operations: 14.8 us -> 1.29 us
  matrix products: 6.88 us -> 0 us
    ppermute x4 -> x0, waiting for transfers between devices: 103 us -> none  [passed_along(): lax.ppermute(shard, axis, [(i, (i + by) % size) for i in range(size)])]
    pallas_call x0 -> x1, Pallas kernels: none -> 74.8 us  [per_device(): pl.pallas_call(functools.partial(tiles_kernel, blocks), out_shape=(out, o...]
    all_gather x1 -> x0, waiting for transfers between devices: 54.2 us -> none  [per_device(): whole = lax.all_gather(series, 'feat', axis=1, tiled=True)]
    exp x2 -> x0, other arithmetic: 16.9 us -> none  [kernel_tile(): return jnp.exp(-dist / denom)]
    ppermute x4 -> x0, starting transfers between devices: 15 us -> none  [passed_along(): lax.ppermute(shard, axis, [(i, (i + by) % size) for i in range(size)])]
    reduce_sum x3 -> x0, other arithmetic: 10.1 us -> none  [the longest x2 8.26 us: kernel_tile(): col_sq = jnp.sum(jnp.square(cols_ext.astype(jnp.float32)), axis=1)]
    all_to_all x1 -> x0, waiting for transfers between devices: 8.09 us -> none  [per_device(): lax.all_to_all(following, 'feat', split_axis=1, concat_axis=0, tiled=True)]
    dot_general x2 -> x0, matrix products: 6.88 us -> none  [kernel_tile(): lax.dot_general(rows_ext, cols_ext, (((1,), (1,)), ((), ())), preferred_e...]
  transfers between devices with their start and end apart: 6 -> 0, of which waited for: 4 -> 0; matrix products, arithmetic and copies ran while one was open for 8% -> 0% of each run, Pallas kernels for 0% -> 0%
where the time goes in v2:
time: 81.1 us; the launch traced here: 81 us
  Pallas kernels  74.8 us (92%)
  local copies, waits for them, and re-layouts  4.14 us (5%)
  between operations  1.29 us (2%)
    pallas_call x1, Pallas kernels, per_device(): pl.pallas_call(functools.partial(tiles_kernel, blocks), out_shape=(out, o...  74.8 us
    unnamed x5, local copies, waits for them, and re-layouts  4.14 us

profile of v2, /device:TPU:1, one launch (start us, length us, event | category | flops | bytes accessed | tf_op | source)
XLA Modules:
  0.0 81.0 jit_solution(3388253719686247980)
XLA Ops:
  1.3 0.7 divide_bitcast_fusion.inv_ref
  2.0 0.0 copy-start
  2.0 1.2 %copy-done = bf16[1024,512]{1,0:T(8,128)(2,1)S(1)} copy-done((bf16[1024,512]{1,0:T(8,128)(2,1)S(1)}, bf16[1024,512]{1,0:T(8,128)(2,1)}, u32[]{:S(2)}) %copy-start) | copy-done | bytes 1048600
  3.2 74.8 %shard_map.58 = (f32[256,1024]{1,0:T(8,128)S(1)}, f32[256,1024]{1,0:T(8,128)S(1)}, f32[256,1024]{1,0:T(8,128)S(1)}) custom-call(bf16[1024,512]{1,0:T(8,128)(2,1)S(1)} %copy-done, f32[8,128]{1,0:T(8,128)S(1)} %divide_bitcast_fusion.inv_ref, f32[1]{0:T(128)S(6)} %copy.9.width_ref), custom_call_target="tpu_custom_call" | custom-call | tf_op jit(solution)/shard_map/pallas_call | solution.py:665
  78.0 1.0 %copy.10 = f32[256,1024]{1,0:T(8,128)} copy(f32[256,1024]{1,0:T(8,128)S(1)} %get-tuple-element.6) | data formatting | bytes 2097152
  79.0 1.0 %copy.11 = f32[256,1024]{1,0:T(8,128)} copy(f32[256,1024]{1,0:T(8,128)S(1)} %get-tuple-element.7) | data formatting | bytes 2097152
  80.0 1.0 %copy.12 = f32[256,1024]{1,0:T(8,128)} copy(f32[256,1024]{1,0:T(8,128)S(1)} %get-tuple-element.8) | data formatting | bytes 2097152
Async XLA Ops:
  2.0 1.2 %copy-start = (bf16[1024,512]{1,0:T(8,128)(2,1)S(1)}, bf16[1024,512]{1,0:T(8,128)(2,1)}, u32[]{:S(2)}) copy-start(bf16[1024,512]{1,0:T(8,128)(2,1)} %series_ref.1) | copy-start | bytes 3145732

commit v3 on v2

v3 whole, which is shorter than its diff:
```python
import functools

import jax
import jax.numpy as jnp
from jax import lax
from jax.experimental import pallas as pl
from jax.experimental.pallas import tpu as pltpu
from jax.sharding import PartitionSpec as P

LAGS = 24
LEAD = 32
LANE = 128
CHUNKS = 8
PIECES = 8
PARTS = 2
MESH = pl.DeviceIdType.MESH
CONTRACT_LAST = (((1,), (1,)), ((), ()))


def multiple(value, of):
    return pl.multiple_of(value, of)


def tiles_kernel(
    blocks,
    series_ref,
    inv_ref,
    width_ref,
    same_ref,
    next_ref,
    prev_ref,
    whole,
    rows,
    nrows,
    mrows,
    mrows_rest,
    ninv,
    minv,
    gram,
    mgram,
    same_gram,
    sums,
    partial,
    squared,
    past_squared,
    lagged,
    nlagged,
    mlagged,
    norms,
    row_norms,
    row_factor,
    kept,
    mkept,
    turned,
    mturned,
    kept_rest,
    mkept_rest,
    turned_rest,
    mturned_rest,
    hop,
    turn_hop,
    mturn_hop,
    rest_hop,
    mrest_hop,
    tail_send,
    tail_recv,
    sib_send,
    sib_recv,
    hop_send,
    hop_recv,
    far_send,
    far_recv,
    pass_send,
    pass_recv,
    lead_send,
    lead_recv,
    inv_send,
    inv_recv,
    square_send,
    square_recv,
    turn_send,
    turn_recv,
    turn_hop_send,
    turn_hop_recv,
    rest_send,
    rest_recv,
    rest_hop_send,
    rest_hop_recv,
    n_send,
    n_recv,
    m_send,
    m_recv,
    k_send,
    k_recv,
    mk_send,
    mk_recv,
    ride_send,
):
    block, quarter = series_ref.shape
    dims = 4 * quarter
    share = block // 4
    part_rows = share // 2
    wide = block + LANE
    past = wide - LEAD

    b, f = lax.axis_index("blk"), lax.axis_index("feat")
    core, chip = lax.rem(f, 2), f // 2
    sib, far, cross = f + 1 - 2 * core, lax.rem(f + 2, 4), 3 - f
    after, before = lax.rem(b + 1, blocks), lax.rem(b + blocks - 1, blocks)
    half = blocks // 2
    pos, first = lax.rem(b, half), (b // half) * half
    over = lax.rem(b + half, blocks)
    others = (sib, far, cross)
    everyone = (f, sib, far, cross)
    near, end = first, first + half - 1
    is_near, is_end = pos == 0, pos == half - 1
    is_seam = jnp.logical_or(is_near, is_end)
    ordinary = jnp.logical_not(is_seam)

    barrier = pltpu.get_barrier_semaphore()
    peers = [(b, j) for j in others] + [(after, f), (before, f)] + [(over, j) for j in (f, far, sib)]
    for peer in peers:
        pl.semaphore_signal(barrier, inc=1, device_id=peer, device_id_type=MESH)

    def greet(condition, corners):
        @pl.when(condition)
        def _():
            for corner in corners:
                pl.semaphore_signal(barrier, inc=1, device_id=corner, device_id_type=MESH)
            pl.semaphore_wait(barrier, len(peers) + len(corners))

    greet(is_near, [(end, f), (end, sib)])
    greet(is_end, [(near, f), (near, sib)])

    @pl.when(ordinary)
    def _():
        pl.semaphore_wait(barrier, len(peers))

    sent = []

    def copy_of(src, dst, send_sem, recv_sem, to):
        return pltpu.make_async_remote_copy(
            src_ref=src, dst_ref=dst, send_sem=send_sem, recv_sem=recv_sem, device_id=to, device_id_type=MESH
        )

    def post(src, dst, send_sem, recv_sem, to):
        copy_of(src, dst, send_sem, recv_sem, to).start()

    def leaves(src, send_sem, recv_sem, condition=None):
        sent.append((condition, copy_of(src, src, send_sem, recv_sem, (b, sib))))

    def send(src, dst, send_sem, recv_sem, to):
        post(src, dst, send_sem, recv_sem, to)
        leaves(src, send_sem, recv_sem)

    def receive(dst, send_sem, recv_sem, sender):
        copy_of(dst, dst, send_sem, recv_sem, sender).wait_recv()

    def when(condition, act):
        @pl.when(condition)
        def _():
            act()

    def cols(q):
        return pl.ds(multiple(q * quarter, quarter), quarter)

    def group(g):
        return pl.ds(multiple(g * share, share), share)

    def n_spot(p):
        return nrows.at[pl.ds(LEAD + (p % 2) * part_rows, part_rows), cols(everyone[p // 2])]

    def m_spot(p):
        size = part_rows // 2
        return mrows.at[pl.ds(LEAD + (p % 2) * size, size), cols(everyone[p // 2])]

    def k_spot(p):
        g, h = p % 4, p // 4
        return prev_ref.at[pl.ds(h * part_rows, part_rows), pl.ds(g * share + part_rows, part_rows)]

    def mk_spot(p):
        size = part_rows // PARTS
        return next_ref.at[pl.ds(p * size, size), :]

    quarter_rows = share // 4

    def own_rows(ref, start, size, columns):
        return ref.at[pl.ds(multiple(f * share + start, size), size), columns]

    def send_n(ref, qi, columns, condition):
        for p in (2 * qi, 2 * qi + 1):
            piece = own_rows(ref, (p % 2) * part_rows, part_rows, columns)
            when(condition, functools.partial(post, piece, n_spot(p), n_send.at[p], n_recv.at[p], (before, f)))

    def send_n_quarter(qi, i, condition):
        p, columns = 2 * qi + i // 2, cols(everyone[qi])
        piece = own_rows(whole, i * quarter_rows, quarter_rows, columns)
        spot = nrows.at[pl.ds(LEAD + i * quarter_rows, quarter_rows), columns]
        when(condition, functools.partial(post, piece, spot, n_send.at[p], n_recv.at[p], (before, f)))

    def send_m(ref, qi, columns, condition, pieces=(0, 1)):
        for i in pieces:
            p = 2 * qi + i
            piece = own_rows(ref, i * quarter_rows, quarter_rows, columns)
            when(condition, functools.partial(post, piece, m_spot(p), m_send.at[p], m_recv.at[p], (after, f)))

    def await_n(p):
        receive(n_spot(p), n_send.at[p], n_recv.at[p], (after, f))

    def await_m(p):
        receive(m_spot(p), m_send.at[p], m_recv.at[p], (before, f))

    has_n, has_m = jnp.logical_not(is_near), jnp.logical_not(is_end)

    def order(c, j):
        return j + c * (2, 2, -1, -3)[j]

    def place_of(k):
        return (k // 2 + 3) % 4

    def halved(sender, k, s):
        c = sender if s == 0 else 1 - sender
        usual = order(1 - sender, k // 2) * share + (k % 2) * 2 * quarter_rows + s * quarter_rows
        at_seam = (2 * c + k % 2) * share + place_of(k) * quarter_rows
        return pl.ds(multiple(jnp.where(is_seam, at_seam, usual), quarter_rows), quarter_rows)

    send(
        series_ref.at[pl.ds(block - LEAD, LEAD), :],
        whole.at[pl.ds(past, LEAD), cols(f)],
        tail_send.at[0],
        tail_recv.at[0],
        (after, f),
    )

    def set_out(k):
        for s, j in enumerate((f, far)):
            i = CHUNKS * s + k
            send(series_ref.at[halved(chip, k, s), :], hop.at[s, k], hop_send.at[i], hop_recv.at[i], (over, j))

    def hand_over(k):
        for s, j in enumerate((f, far)):
            i = CHUNKS * s + k
            receive(hop.at[s, k], hop_send.at[i], hop_recv.at[i], (over, j))
            c, to = (chip, far) if s == 0 else (1 - chip, f)
            send(hop.at[s, k], whole.at[halved(c, k, s), cols(j)], far_send.at[i], far_recv.at[i], (over, to))

            to, place = 2 * chip + k % 2, place_of(k)
            qi = lax.rem(core + k % 2, 2) + 2 * s
            spot = pl.ds(LEAD + place * quarter_rows, quarter_rows)

            def ride_back():
                post(
                    hop.at[s, k], nrows.at[spot, cols(j)], ride_send.at[i], n_recv.at[2 * qi + place // 2], (end, to)
                )

            def ride_on():
                at = pl.ds(LEAD + (place % 2) * quarter_rows, quarter_rows)
                rows_there = mrows if place < 2 else mrows_rest
                sem = m_recv.at[2 * qi + place] if place < 2 else rest_recv.at[6 + 2 * qi + place - 2]
                post(hop.at[s, k], rows_there.at[at, cols(j)], ride_send.at[i], sem, (near, to))

            when(is_near, ride_back)
            leaves(hop.at[s, k], ride_send.at[i], n_recv.at[0], is_near)
            when(is_end, ride_on)
            leaves(hop.at[s, k], ride_send.at[i], n_recv.at[0], is_end)

    set_out(0)
    set_out(1)
    send(series_ref, whole.at[pl.ds(0, block), cols(f)], sib_send.at[0], sib_recv.at[0], (b, sib))
    send_n(series_ref, 0, slice(None), has_n)
    send_m(series_ref, 0, slice(None), has_m)
    send(inv_ref, ninv, inv_send.at[0], inv_recv.at[0], (before, f))
    send(inv_ref, minv, inv_send.at[1], inv_recv.at[1], (after, f))

    whole[pl.ds(0, block), cols(f)] = series_ref[...]
    whole[pl.ds(block, LANE - LEAD), :] = jnp.zeros((LANE - LEAD, dims), whole.dtype)
    for buffer in (gram, mgram, same_gram):
        buffer[pl.ds(0, 8), :] = jnp.zeros((8, wide), jnp.float32)

    def pass_on(k):
        for s in range(2):
            i = CHUNKS * s + k
            piece = whole.at[halved(1 - chip, k, s), cols(far)]
            receive(piece, far_send.at[i], far_recv.at[i], (over, far if s == 0 else f))
            send(piece, piece, pass_send.at[i], pass_recv.at[i], (b, sib))

    def passed(k):
        for s in range(2):
            i = CHUNKS * s + k
            piece = whole.at[halved(1 - chip, k, s), cols(cross)]
            receive(piece, pass_send.at[i], pass_recv.at[i], (b, sib))

    lead = multiple(lax.rem(f * share + wide - LEAD, wide), LEAD)
    near_half = pl.ds(multiple(chip * 2 * quarter, quarter), 2 * quarter)
    far_half = pl.ds(multiple((1 - chip) * 2 * quarter, quarter), 2 * quarter)
    leads = (near_half, far_half)
    lead_ways = ((nrows, before, after), (mrows, after, before))

    def post_lead(i):
        for w, (dst, to, _) in enumerate(lead_ways):
            s = 2 * w + i
            post(
                whole.at[pl.ds(lead, LEAD), leads[i]],
                dst.at[pl.ds(0, LEAD), leads[i]],
                lead_send.at[s],
                lead_recv.at[s],
                (to, f),
            )

    def receive_lead(w, i):
        dst, _, sender = lead_ways[w]
        receive(dst.at[pl.ds(0, LEAD), leads[i]], lead_send.at[2 * w + i], lead_recv.at[2 * w + i], (sender, f))

    lines = block // LANE

    def square_lines(lines_now):
        for j in lines_now:
            x = whole[pl.ds(j * LANE, LANE), cols(f)]
            total = jnp.zeros((LANE, LANE), jnp.float32)
            for g in range(quarter // LANE):
                piece = x[:, g * LANE : (g + 1) * LANE].astype(jnp.float32)
                total = total + piece * piece
            partial[pl.ds(f, 1), pl.ds(j, 1), :] = jnp.sum(total.T, axis=0, keepdims=True)[None]

    def share_squares():
        for i, j in enumerate(others):
            send(partial.at[f], partial.at[f], square_send.at[i], square_recv.at[i], (b, j))

    def sum_squares():
        for i, j in enumerate(others):
            receive(partial.at[j], square_send.at[i], square_recv.at[i], (b, j))
        squared[...] = partial[0] + partial[1] + partial[2] + partial[3]
        send(squared, past_squared, square_send.at[3], square_recv.at[3], (after, f))

    def lag_squares():
        receive(past_squared, square_send.at[3], square_recv.at[3], (before, f))
        line = [squared[j : j + 1, :] for j in range(lines)] + [past_squared[lines - 1 : lines, :]]
        norms[...] = lag_sum(jnp.broadcast_to(jnp.concatenate(line, axis=1), (8, wide)), 1)
        for j in range(lines):
            lagged[j : j + 1, :] = norms[0:1, j * LANE : (j + 1) * LANE]
        send(lagged, nlagged, square_send.at[4], square_recv.at[4], (before, f))
        send(lagged, mlagged, square_send.at[5], square_recv.at[5], (after, f))

    def lag_sum(x, axis):
        for step in (1, 2, 4):
            x = x + pltpu.roll(x, step, axis)
        return x + pltpu.roll(x, 8, axis) + pltpu.roll(x, 16, axis)

    def products(left, right):
        return lax.dot_general(left, right, CONTRACT_LAST, preferred_element_type=jnp.float32)

    def same_products(start, size):
        part = pl.ds(multiple(start, LANE), size)
        same_gram[pl.ds(8, LEAD + share), part] = products(rows[...], whole[part, :])

    def add_products(target, source, which, fresh):
        size, height = 256, source.shape[0]
        for start in range(0, wide, size):
            part = pl.ds(start, min(size, wide - start))
            found = products(source[:, which], whole[part, which])
            if fresh:
                target[pl.ds(8, height), part] = found
            else:
                target[pl.ds(8, height), part] += found

    def near_products():
        for p in range(4):
            await_n(p)
        receive_lead(0, 0)
        add_products(gram, nrows, near_half, True)

    both = jnp.logical_and
    first_core, second_core = both(ordinary, core == 0), both(ordinary, core == 1)
    for k in range(CHUNKS):
        hand_over(k)
        if k + 2 < CHUNKS:
            set_out(k + 2)
        if k == 0:
            receive(whole.at[pl.ds(0, block), cols(sib)], sib_send.at[0], sib_recv.at[0], (b, sib))
            send_n(whole, 1, cols(sib), has_n)
            send_m(whole, 1, cols(sib), has_m)
            tail = whole.at[pl.ds(past, LEAD), cols(f)]
            receive(tail, tail_send.at[0], tail_recv.at[0], (before, f))
            for i, j in enumerate(others):
                send(tail, tail, tail_send.at[1 + i], tail_recv.at[1 + i], (b, j))
            square_lines(range(lines // 2))
        else:
            pass_on(k - 1)
        if k == 1:
            square_lines(range(lines // 2, lines))
            share_squares()
        if k == 2:
            for i, j in enumerate(others):
                receive(whole.at[pl.ds(past, LEAD), cols(j)], tail_send.at[1 + i], tail_recv.at[1 + i], (b, j))
            post_lead(0)
            send_n(whole, 2, cols(far), first_core)
            send_m(whole, 2, cols(far), first_core)
            send_n_quarter(2, place_of(0), is_end)
            sum_squares()
        if k == 3:
            send_m(whole, 2, cols(far), second_core)
            passed(0)
            passed(1)
            send_n(whole, 3, cols(cross), first_core)
            send_m(whole, 3, cols(cross), first_core)
            send_n_quarter(3, place_of(0), is_end)
            when(is_seam, lambda: post_lead(1))
            lag_squares()
        if k == 4:
            send_n(whole, 2, cols(far), second_core)
            passed(2)
            send_m(whole, 3, cols(cross), second_core)
            send_n_quarter(2, place_of(2), is_end)
            send_m(whole, 2, cols(far), is_near, (0,))
        if k == 5:
            passed(3)
            send_n(whole, 3, cols(cross), second_core)
            send_n_quarter(3, place_of(2), is_end)
            send_m(whole, 3, cols(cross), is_near, (0,))
        if k == 6:
            send_n_quarter(2, place_of(4), is_end)
            send_m(whole, 2, cols(far), is_near, (1,))
            for p in range(4):
                await_m(p)
            receive_lead(1, 0)
            add_products(mgram, mrows, near_half, True)
        if k == 7:
            passed(4)
            passed(5)
            send_n_quarter(3, place_of(4), is_end)
            send_m(whole, 3, cols(cross), is_near, (1,))
            when(ordinary, lambda: post_lead(1))
            when(jnp.logical_not(is_end), near_products)
    pass_on(7)
    send_n_quarter(2, place_of(6), is_end)
    passed(6)
    passed(7)
    send_n_quarter(3, place_of(6), is_end)
    for i in range(2):
        for w in range(2):
            leaves(whole.at[pl.ds(lead, LEAD), leads[i]], lead_send.at[2 * w + i], lead_recv.at[2 * w + i])
    for p in range(8):
        leaves(n_spot(p), n_send.at[p], n_recv.at[p], has_n)
        leaves(m_spot(p), m_send.at[p], m_recv.at[p], has_m)
    when(is_end, near_products)

    inv_row = jnp.concatenate([inv_ref[j : j + 1, :] for j in range(block // LANE)], axis=1)
    width_row = jnp.full((1, LANE), width_ref[0], jnp.float32) * (LAGS * dims)

    def down(line):
        return jnp.broadcast_to(line, (LANE, LANE)).T

    def row_values(inv, squares, count, skip=0):
        for j in range(count // LANE):
            line, part = pl.ds(f * (share // LANE) + skip + j, 1), pl.ds(j * LANE, LANE)
            row_factor[part, :] = down(-inv[line, :] / width_row)
            row_norms[part, :] = down(squares[line, :])

    def all_columns(x):
        return x[:, :block]

    def first_halves(x):
        return jnp.concatenate([x[:, g * share : g * share + part_rows] for g in range(4)], axis=1)

    def second_halves(x):
        return jnp.concatenate([x[:, g * share + part_rows : (g + 1) * share] for g in range(4)], axis=1)

    def tile(products_of, target, pick, parts, ready):
        per = target.shape[0] // 32 // parts
        for h in range(parts):
            for t in range(h * per + 1 if h else 0, (h + 1) * per + 1):
                x = products_of[pl.ds(t * 32, 40), :]
                for step in (1, 2, 4):
                    x = x + pltpu.roll(pltpu.roll(x, step, 0), step, 1)
                sums[pl.ds(t * 32, 32), :] = x[8:, :]
            for t in range(h * per, (h + 1) * per):
                x = sums[pl.ds(t * 32 + 32, 32), :]
                x = x + pltpu.roll(sums[pl.ds(t * 32 + 24, 32), :], 8, 1)
                x = x + pltpu.roll(sums[pl.ds(t * 32 + 16, 32), :], 16, 1)
                part = pl.ds(t * 32, 32)
                spread = row_norms[part, :][:, :1] + pick(norms[pl.ds(0, 1), :]) - 2.0 * pick(x)
                target[part, :] = jnp.exp(spread * (row_factor[part, :][:, :1] * pick(inv_row)))
            ready(h)

    receive(minv, inv_send.at[1], inv_recv.at[1], (before, f))
    receive(ninv, inv_send.at[0], inv_recv.at[0], (after, f))
    receive(nlagged, square_send.at[4], square_recv.at[4], (after, f))
    receive(mlagged, square_send.at[5], square_recv.at[5], (before, f))
    row_values(minv, mlagged, part_rows)
    for p in range(4, 8):
        await_m(p)
    receive_lead(1, 1)
    add_products(mgram, mrows, far_half, False)

    def send_mk(h):
        piece = mkept.at[pl.ds(h * (part_rows // PARTS), part_rows // PARTS), :]
        when(has_n, functools.partial(post, piece, mk_spot(h), mk_send.at[h], mk_recv.at[h], (before, f)))
        leaves(piece, mk_send.at[h], mk_recv.at[h], has_n)

    tile(mgram, mkept, all_columns, PARTS, send_mk)

    my_columns = pl.ds(multiple(f * share, share), share)
    my_first = pl.ds(multiple(f * share, part_rows), part_rows)
    lower = pl.ds(part_rows, part_rows)
    hops = ((0, far, f), (1, cross, far))

    def own_transposed(source):
        lines = [source[:, pl.ds(multiple(f * share + i * LANE, LANE), LANE)].T for i in range(share // LANE)]
        return jnp.concatenate(lines, axis=0)

    def turn_m(j):
        for i in range(share // LANE):
            part = pl.ds(multiple(j * share + i * LANE, LANE), LANE)
            mturned[part, :] = mkept[:, part].T

    for s, j, by in hops:
        turn_m(j)
        send(mturned.at[group(j), :], mturn_hop.at[s], turn_hop_send.at[2 + s], turn_hop_recv.at[2 + s], (over, by))
    turn_m(sib)
    send(mturned.at[group(sib), :], prev_ref.at[:, my_first], turn_send.at[5], turn_recv.at[5], (b, sib))
    prev_ref[:, my_first] = own_transposed(mkept)

    row_values(ninv, nlagged, share)
    for p in range(4, 8):
        await_n(p)
    receive_lead(0, 1)
    add_products(gram, nrows, far_half, False)

    def send_k(h):
        for g in range(4):
            piece, p = kept.at[pl.ds(h * part_rows, part_rows), pl.ds(g * part_rows, part_rows)], 4 * h + g
            when(has_m, functools.partial(post, piece, k_spot(p), k_send.at[p], k_recv.at[p], (after, f)))
            leaves(piece, k_send.at[p], k_recv.at[p], has_m)

    tile(gram, kept, second_halves, PARTS, send_k)

    def seconds(j):
        return pl.ds(multiple(j * part_rows, part_rows), part_rows)

    def turn(j):
        turned[seconds(j), :] = kept[:, seconds(j)].T

    for s, j, by in hops:
        turn(j)
        send(turned.at[seconds(j), :], turn_hop.at[s], turn_hop_send.at[s], turn_hop_recv.at[s], (over, by))
    turn(sib)
    send(turned.at[seconds(sib), :], next_ref.at[lower, my_columns], turn_send.at[2], turn_recv.at[2], (b, sib))
    next_ref[lower, my_columns] = kept[:, seconds(f)].T

    def firsts_of(j):
        return pl.ds(multiple(j * share, part_rows), part_rows)

    for s, j, to in ((0, f, far), (1, far, sib)):
        receive(mturn_hop.at[s], turn_hop_send.at[2 + s], turn_hop_recv.at[2 + s], (over, j))
        send(mturn_hop.at[s], prev_ref.at[:, firsts_of(j)], turn_send.at[3 + s], turn_recv.at[3 + s], (over, to))

    upper = pl.ds(0, part_rows)

    def rest_of_next():
        tile(gram, kept_rest, first_halves, 1, lambda h: None)
        for s, j, by in hops:
            turned_rest[seconds(j), :] = kept_rest[:, seconds(j)].T
            post(turned_rest.at[seconds(j), :], rest_hop.at[s], rest_hop_send.at[s], rest_hop_recv.at[s], (over, by))
        turned_rest[seconds(sib), :] = kept_rest[:, seconds(sib)].T
        post(
            turned_rest.at[seconds(sib), :],
            next_ref.at[upper, my_columns],
            rest_send.at[2],
            rest_recv.at[2],
            (b, sib),
        )
        next_ref[upper, my_columns] = kept_rest[:, seconds(f)].T
        for s, j, to in ((0, f, far), (1, far, sib)):
            receive(rest_hop.at[s], rest_hop_send.at[s], rest_hop_recv.at[s], (over, j))
            post(rest_hop.at[s], next_ref.at[upper, group(j)], rest_send.at[s], rest_recv.at[s], (over, to))

    def rest_of_prev():
        for qi in range(4):
            for i in range(2):
                sem = 6 + 2 * qi + i
                spot = mrows_rest.at[pl.ds(LEAD + i * quarter_rows, quarter_rows), cols(everyone[qi])]
                receive(spot, rest_send.at[sem], rest_recv.at[sem], (before, f))
        mrows_rest[pl.ds(0, LEAD), :] = mrows[pl.ds(part_rows, LEAD), :]
        add_products(mgram, mrows_rest, slice(None), True)
        row_values(minv, mlagged, part_rows, 1)
        tile(mgram, mkept_rest, all_columns, 1, lambda h: None)
        for s, j, by in hops:
            turn_rest(j)
            post(mturned_rest.at[group(j), :], mrest_hop.at[s], rest_hop_send.at[s], rest_hop_recv.at[s], (over, by))
        turn_rest(sib)
        post(mturned_rest.at[group(sib), :], prev_ref.at[:, my_second], rest_send.at[5], rest_recv.at[5], (b, sib))
        prev_ref[:, my_second] = own_transposed(mkept_rest)
        for s, j, to in ((0, f, far), (1, far, sib)):
            receive(mrest_hop.at[s], rest_hop_send.at[s], rest_hop_recv.at[s], (over, j))
            post(mrest_hop.at[s], prev_ref.at[:, seconds_of(j)], rest_send.at[3 + s], rest_recv.at[3 + s], (over, to))

    def turn_rest(j):
        for i in range(share // LANE):
            part = pl.ds(multiple(j * share + i * LANE, LANE), LANE)
            mturned_rest[part, :] = mkept_rest[:, part].T

    def seconds_of(j):
        return pl.ds(multiple(j * share + part_rows, part_rows), part_rows)

    my_second = seconds_of(f)
    when(is_end, rest_of_next)
    when(is_near, rest_of_prev)

    rows[pl.ds(0, LEAD), :] = whole[pl.ds(lead, LEAD), :]
    rows[pl.ds(LEAD, share), :] = whole[group(f), :]
    for j in range(4):
        same_products(order(chip, j) * share, share)
    same_products(block, LANE)
    row_values(inv_ref, lagged, share)

    def between(h):
        if h == 0:
            for s, j, to in ((0, f, far), (1, far, sib)):
                receive(turn_hop.at[s], turn_hop_send.at[s], turn_hop_recv.at[s], (over, j))
                send(turn_hop.at[s], next_ref.at[lower, group(j)], turn_send.at[s], turn_recv.at[s], (over, to))

    tile(same_gram, same_ref, all_columns, PARTS, between)

    def await_mk():
        for p in range(PARTS):
            receive(mk_spot(p), mk_send.at[p], mk_recv.at[p], (after, f))

    def await_k():
        for p in range(4 * PARTS):
            receive(k_spot(p), k_send.at[p], k_recv.at[p], (before, f))

    when(has_m, await_mk)
    when(has_n, await_k)

    def await_rest(i, dst, source):
        receive(dst, rest_send.at[i], rest_recv.at[i], (b, source))

    for i, j in enumerate((far, cross, sib)):
        when(is_end, functools.partial(await_rest, i, next_ref.at[upper, group(j)], j))
        when(is_near, functools.partial(await_rest, 3 + i, prev_ref.at[:, seconds_of(j)], j))
    for s in range(2):
        leaves(rest_hop.at[s], rest_hop_send.at[s], rest_hop_recv.at[s], is_seam)
        leaves(rest_hop.at[s], rest_send.at[s], rest_recv.at[s], is_end)
        leaves(mrest_hop.at[s], rest_send.at[3 + s], rest_recv.at[3 + s], is_near)
    leaves(turned_rest.at[seconds(sib), :], rest_send.at[2], rest_recv.at[2], is_end)
    leaves(mturned_rest.at[group(sib), :], rest_send.at[5], rest_recv.at[5], is_near)
    for i, j in enumerate((far, cross, sib)):
        receive(next_ref.at[lower, group(j)], turn_send.at[i], turn_recv.at[i], (b, j))
        receive(prev_ref.at[:, firsts_of(j)], turn_send.at[3 + i], turn_recv.at[3 + i], (b, j))
    for condition, copy in sent:
        if condition is None:
            copy.wait_send()
        else:
            when(condition, copy.wait_send)


def per_device(blocks, series, scales, width):
    block, quarter = series.shape
    dims, share, wide = 4 * quarter, block // 4, block + LANE
    part_rows = share // 2
    inv = (1.0 / scales.astype(jnp.float32)).reshape(block // LANE, LANE)
    out = jax.ShapeDtypeStruct((share, block), jnp.float32)
    raw = lambda *shape: pltpu.VMEM(shape, series.dtype)
    wider = lambda *shape: pltpu.VMEM(shape, jnp.float32)
    hops = 2 * CHUNKS
    pairs = (4, 1, hops, hops, hops, 4, 2, 6, 6, 4, 14, 2, PIECES, PIECES, 4 * PARTS, PARTS)
    counts = [n for n in pairs for _ in range(2)] + [hops]
    return pl.pallas_call(
        functools.partial(tiles_kernel, blocks),
        out_shape=(out, out, out),
        in_specs=[
            pl.BlockSpec(memory_space=pltpu.VMEM),
            pl.BlockSpec(memory_space=pltpu.VMEM),
            pl.BlockSpec(memory_space=pltpu.SMEM),
        ],
        out_specs=(pl.BlockSpec(memory_space=pltpu.VMEM),) * 3,
        scratch_shapes=[
            raw(wide, dims),
            raw(LEAD + share, dims),
            raw(LEAD + share, dims),
            raw(LEAD + part_rows, dims),
            raw(LEAD + part_rows, dims),
            wider(block // LANE, LANE),
            wider(block // LANE, LANE),
            wider(8 + LEAD + share, wide),
            wider(8 + LEAD + part_rows, wide),
            wider(8 + LEAD + share, wide),
            wider(LEAD + share, wide),
            wider(4, block // LANE, LANE),
        ]
        + [wider(block // LANE, LANE)] * 5
        + [
            wider(8, wide),
            wider(share, LANE),
            wider(share, LANE),
            wider(share, block // 2),
            wider(part_rows, block),
            wider(block // 2, share),
            wider(block, part_rows),
            wider(share, block // 2),
            wider(part_rows, block),
            wider(block // 2, share),
            wider(block, part_rows),
            raw(2, CHUNKS, 2 * share // CHUNKS, quarter),
            wider(2, part_rows, share),
            wider(2, share, part_rows),
            wider(2, part_rows, share),
            wider(2, share, part_rows),
        ]
        + [pltpu.SemaphoreType.DMA((n,)) for n in counts],
        compiler_params=pltpu.CompilerParams(
            collective_id=0, has_side_effects=True, vmem_limit_bytes=48 * 1024 * 1024
        ),
    )(series, inv, width)


def solution(mesh):
    in_specs = (P("blk", "feat"), P("blk"), P())
    out_specs = (P(("blk", "feat"), None), P(("blk", "feat"), None), P(("blk", "feat"), None))
    return jax.shard_map(
        functools.partial(per_device, mesh.shape["blk"]),
        mesh=mesh,
        in_specs=in_specs,
        out_specs=out_specs,
        check_vma=False,
    )
```

time: 81.1 us -> 80.1 us (0.988)
  Pallas kernels: 74.8 us -> 73.8 us
    pallas_call x1, Pallas kernels: 74.8 us -> 73.8 us  [per_device(): pl.pallas_call(functools.partial(tiles_kernel, blocks), out_shape=(out, o...]
where the time goes in v3:
time: 80.1 us; the launch traced here: 79.9 us
  Pallas kernels  73.8 us (92%)
  local copies, waits for them, and re-layouts  4.14 us (5%)
  between operations  1.29 us (2%)
    pallas_call x1, Pallas kernels, per_device(): pl.pallas_call(functools.partial(tiles_kernel, blocks), out_shape=(out, o...  73.8 us
    unnamed x5, local copies, waits for them, and re-layouts  4.14 us

profile of v3, /device:TPU:1, one launch (start us, length us, event | category | flops | bytes accessed | tf_op | source)
XLA Modules:
  0.0 79.9 jit_solution(11434925682708856034)
XLA Ops:
  1.3 0.7 divide_bitcast_fusion.inv_ref
  2.0 0.0 copy-start
  2.0 1.2 %copy-done = bf16[1024,512]{1,0:T(8,128)(2,1)S(1)} copy-done((bf16[1024,512]{1,0:T(8,128)(2,1)S(1)}, bf16[1024,512]{1,0:T(8,128)(2,1)}, u32[]{:S(2)}) %copy-start) | copy-done | bytes 1048600
  3.2 73.8 %shard_map.58 = (f32[256,1024]{1,0:T(8,128)S(1)}, f32[256,1024]{1,0:T(8,128)S(1)}, f32[256,1024]{1,0:T(8,128)S(1)}) custom-call(bf16[1024,512]{1,0:T(8,128)(2,1)S(1)} %copy-done, f32[8,128]{1,0:T(8,128)S(1)} %divide_bitcast_fusion.inv_ref, f32[1]{0:T(128)S(6)} %copy.9.width_ref), custom_call_target="tpu_custom_call" | custom-call | tf_op jit(solution)/shard_map/pallas_call | solution.py:668
  77.0 1.0 %copy.10 = f32[256,1024]{1,0:T(8,128)} copy(f32[256,1024]{1,0:T(8,128)S(1)} %get-tuple-element.6) | data formatting | bytes 2097152
  78.0 1.0 %copy.11 = f32[256,1024]{1,0:T(8,128)} copy(f32[256,1024]{1,0:T(8,128)S(1)} %get-tuple-element.7) | data formatting | bytes 2097152
  78.9 1.0 %copy.12 = f32[256,1024]{1,0:T(8,128)} copy(f32[256,1024]{1,0:T(8,128)S(1)} %get-tuple-element.8) | data formatting | bytes 2097152
Async XLA Ops:
  2.0 1.2 %copy-start = (bf16[1024,512]{1,0:T(8,128)(2,1)S(1)}, bf16[1024,512]{1,0:T(8,128)(2,1)}, u32[]{:S(2)}) copy-start(bf16[1024,512]{1,0:T(8,128)(2,1)} %series_ref.1) | copy-start | bytes 3145732

commit v4 on v3

--- a/solution.py
+++ b/solution.py
@@ -349,9 +349,9 @@
     def products(left, right):
         return lax.dot_general(left, right, CONTRACT_LAST, preferred_element_type=jnp.float32)
 
-    def same_products(start, size):
-        part = pl.ds(multiple(start, LANE), size)
-        same_gram[pl.ds(8, LEAD + share), part] = products(rows[...], whole[part, :])
+    def own_group(which):
+        rows[pl.ds(0, LEAD), which] = whole[pl.ds(lead, LEAD), which]
+        rows[pl.ds(LEAD, share), which] = whole[group(f), which]
 
     def add_products(target, source, which, fresh):
         size, height = 256, source.shape[0]
@@ -412,6 +412,8 @@
             send_m(whole, 3, cols(cross), second_core)
             send_n_quarter(2, place_of(2), is_end)
             send_m(whole, 2, cols(far), is_near, (0,))
+            own_group(near_half)
+            add_products(same_gram, rows, near_half, True)
         if k == 5:
             passed(3)
             send_n(whole, 3, cols(cross), second_core)
@@ -456,30 +458,45 @@
             row_factor[part, :] = down(-inv[line, :] / width_row)
             row_norms[part, :] = down(squares[line, :])
 
-    def all_columns(x):
-        return x[:, :block]
-
-    def first_halves(x):
-        return jnp.concatenate([x[:, g * share : g * share + part_rows] for g in range(4)], axis=1)
-
-    def second_halves(x):
-        return jnp.concatenate([x[:, g * share + part_rows : (g + 1) * share] for g in range(4)], axis=1)
+    middle = block // 2
+
+    def with_lead(ref, part, c):
+        if c:
+            return ref[part, middle - LANE : block]
+        return jnp.concatenate([ref[part, block:wide], ref[part, :middle]], axis=1)
+
+    def all_columns(c):
+        return [(c * middle, middle)]
+
+    def first_halves(c):
+        return [(g * share, part_rows) for g in (2 * c, 2 * c + 1)]
+
+    def second_halves(c):
+        return [(g * share + part_rows, part_rows) for g in (2 * c, 2 * c + 1)]
 
     def tile(products_of, target, pick, parts, ready):
         per = target.shape[0] // 32 // parts
+        span = target.shape[1] // 2
         for h in range(parts):
-            for t in range(h * per + 1 if h else 0, (h + 1) * per + 1):
-                x = products_of[pl.ds(t * 32, 40), :]
-                for step in (1, 2, 4):
-                    x = x + pltpu.roll(pltpu.roll(x, step, 0), step, 1)
-                sums[pl.ds(t * 32, 32), :] = x[8:, :]
-            for t in range(h * per, (h + 1) * per):
-                x = sums[pl.ds(t * 32 + 32, 32), :]
-                x = x + pltpu.roll(sums[pl.ds(t * 32 + 24, 32), :], 8, 1)
-                x = x + pltpu.roll(sums[pl.ds(t * 32 + 16, 32), :], 16, 1)
-                part = pl.ds(t * 32, 32)
-                spread = row_norms[part, :][:, :1] + pick(norms[pl.ds(0, 1), :]) - 2.0 * pick(x)
-                target[part, :] = jnp.exp(spread * (row_factor[part, :][:, :1] * pick(inv_row)))
+            for c in range(2):
+                for t in range(h * per + 1 if h else 0, (h + 1) * per + 1):
+                    x = with_lead(products_of, pl.ds(t * 32, 40), c)
+                    for step in (1, 2, 4):
+                        x = x + pltpu.roll(pltpu.roll(x, step, 0), step, 1)
+                    part = pl.ds(t * 32, 32)
+                    sums[part, c * middle : (c + 1) * middle] = x[8:, LANE:]
+                    if c == 0:
+                        sums[part, block:wide] = x[8:, :LANE]
+                picked = lambda x, base: jnp.concatenate([x[:, s - base : s - base + n] for s, n in pick(c)], axis=1)
+                for t in range(h * per, (h + 1) * per):
+                    x = with_lead(sums, pl.ds(t * 32 + 32, 32), c)
+                    x = x + pltpu.roll(with_lead(sums, pl.ds(t * 32 + 24, 32), c), 8, 1)
+                    x = x + pltpu.roll(with_lead(sums, pl.ds(t * 32 + 16, 32), c), 16, 1)
+                    part = pl.ds(t * 32, 32)
+                    found = picked(x, c * middle - LANE)
+                    spread = row_norms[part, :][:, :1] + picked(norms[pl.ds(0, 1), :], 0) - 2.0 * found
+                    values = jnp.exp(spread * (row_factor[part, :][:, :1] * picked(inv_row, 0)))
+                    target[part, c * span : (c + 1) * span] = values
             ready(h)
 
     receive(minv, inv_send.at[1], inv_recv.at[1], (before, f))
@@ -549,10 +566,6 @@
 
     def firsts_of(j):
         return pl.ds(multiple(j * share, part_rows), part_rows)
-
-    for s, j, to in ((0, f, far), (1, far, sib)):
-        receive(mturn_hop.at[s], turn_hop_send.at[2 + s], turn_hop_recv.at[2 + s], (over, j))
-        send(mturn_hop.at[s], prev_ref.at[:, firsts_of(j)], turn_send.at[3 + s], turn_recv.at[3 + s], (over, to))
 
     upper = pl.ds(0, part_rows)
 
@@ -570,6 +583,8 @@
             (b, sib),
         )
         next_ref[upper, my_columns] = kept_rest[:, seconds(f)].T
+
+    def relay_rest_of_next():
         for s, j, to in ((0, f, far), (1, far, sib)):
             receive(rest_hop.at[s], rest_hop_send.at[s], rest_hop_recv.at[s], (over, j))
             post(rest_hop.at[s], next_ref.at[upper, group(j)], rest_send.at[s], rest_recv.at[s], (over, to))
@@ -590,6 +605,8 @@
         turn_rest(sib)
         post(mturned_rest.at[group(sib), :], prev_ref.at[:, my_second], rest_send.at[5], rest_recv.at[5], (b, sib))
         prev_ref[:, my_second] = own_transposed(mkept_rest)
+
+    def relay_rest_of_prev():
         for s, j, to in ((0, f, far), (1, far, sib)):
             receive(mrest_hop.at[s], rest_hop_send.at[s], rest_hop_recv.at[s], (over, j))
             post(mrest_hop.at[s], prev_ref.at[:, seconds_of(j)], rest_send.at[3 + s], rest_recv.at[3 + s], (over, to))
@@ -603,14 +620,15 @@
         return pl.ds(multiple(j * share + part_rows, part_rows), part_rows)
 
     my_second = seconds_of(f)
+    for s, j, to in ((0, f, far), (1, far, sib)):
+        receive(mturn_hop.at[s], turn_hop_send.at[2 + s], turn_hop_recv.at[2 + s], (over, j))
+        send(mturn_hop.at[s], prev_ref.at[:, firsts_of(j)], turn_send.at[3 + s], turn_recv.at[3 + s], (over, to))
+
     when(is_end, rest_of_next)
     when(is_near, rest_of_prev)
 
-    rows[pl.ds(0, LEAD), :] = whole[pl.ds(lead, LEAD), :]
-    rows[pl.ds(LEAD, share), :] = whole[group(f), :]
-    for j in range(4):
-        same_products(order(chip, j) * share, share)
-    same_products(block, LANE)
+    own_group(far_half)
+    add_products(same_gram, rows, far_half, False)
     row_values(inv_ref, lagged, share)
 
     def between(h):
@@ -618,6 +636,8 @@
             for s, j, to in ((0, f, far), (1, far, sib)):
                 receive(turn_hop.at[s], turn_hop_send.at[s], turn_hop_recv.at[s], (over, j))
                 send(turn_hop.at[s], next_ref.at[lower, group(j)], turn_send.at[s], turn_recv.at[s], (over, to))
+            when(is_end, relay_rest_of_next)
+            when(is_near, relay_rest_of_prev)
 
     tile(same_gram, same_ref, all_columns, PARTS, between)
 

time: 80.1 us -> 78.5 us (0.980)
  Pallas kernels: 73.8 us -> 72.2 us
    pallas_call x1, Pallas kernels: 73.8 us -> 72.2 us  [per_device(): pl.pallas_call(functools.partial(tiles_kernel, blocks), out_shape=(out, o...]
where the time goes in v4:
time: 78.5 us; the launch traced here: 78.3 us
  Pallas kernels  72.2 us (92%)
  local copies, waits for them, and re-layouts  4.14 us (5%)
  between operations  1.29 us (2%)
    pallas_call x1, Pallas kernels, per_device(): pl.pallas_call(functools.partial(tiles_kernel, blocks), out_shape=(out, o...  72.2 us
    unnamed x5, local copies, waits for them, and re-layouts  4.14 us

profile of v4, /device:TPU:1, one launch (start us, length us, event | category | flops | bytes accessed | tf_op | source)
XLA Modules:
  0.0 78.3 jit_solution(5243900141877609649)
XLA Ops:
  1.3 0.7 divide_bitcast_fusion.inv_ref
  2.0 0.0 copy-start
  2.0 1.2 %copy-done = bf16[1024,512]{1,0:T(8,128)(2,1)S(1)} copy-done((bf16[1024,512]{1,0:T(8,128)(2,1)S(1)}, bf16[1024,512]{1,0:T(8,128)(2,1)}, u32[]{:S(2)}) %copy-start) | copy-done | bytes 1048600
  3.2 72.2 %shard_map.58 = (f32[256,1024]{1,0:T(8,128)S(1)}, f32[256,1024]{1,0:T(8,128)S(1)}, f32[256,1024]{1,0:T(8,128)S(1)}) custom-call(bf16[1024,512]{1,0:T(8,128)(2,1)S(1)} %copy-done, f32[8,128]{1,0:T(8,128)S(1)} %divide_bitcast_fusion.inv_ref, f32[1]{0:T(128)S(6)} %copy.9.width_ref), custom_call_target="tpu_custom_call" | custom-call | tf_op jit(solution)/shard_map/pallas_call | solution.py:688
  75.4 1.0 %copy.10 = f32[256,1024]{1,0:T(8,128)} copy(f32[256,1024]{1,0:T(8,128)S(1)} %get-tuple-element.6) | data formatting | bytes 2097152
  76.3 1.0 %copy.11 = f32[256,1024]{1,0:T(8,128)} copy(f32[256,1024]{1,0:T(8,128)S(1)} %get-tuple-element.7) | data formatting | bytes 2097152
  77.3 1.0 %copy.12 = f32[256,1024]{1,0:T(8,128)} copy(f32[256,1024]{1,0:T(8,128)S(1)} %get-tuple-element.8) | data formatting | bytes 2097152
Async XLA Ops:
  2.0 1.2 %copy-start = (bf16[1024,512]{1,0:T(8,128)(2,1)S(1)}, bf16[1024,512]{1,0:T(8,128)(2,1)}, u32[]{:S(2)}) copy-start(bf16[1024,512]{1,0:T(8,128)(2,1)} %series_ref.1) | copy-start | bytes 3145732

commit v5 on v4

--- a/solution.py
+++ b/solution.py
@@ -13,6 +13,7 @@
 CHUNKS = 8
 PIECES = 8
 PARTS = 2
+AHEAD = 4
 MESH = pl.DeviceIdType.MESH
 CONTRACT_LAST = (((1,), (1,)), ((), ()))
 
@@ -264,8 +265,8 @@
             when(is_end, ride_on)
             leaves(hop.at[s, k], ride_send.at[i], n_recv.at[0], is_end)
 
-    set_out(0)
-    set_out(1)
+    for k in range(AHEAD):
+        set_out(k)
     send(series_ref, whole.at[pl.ds(0, block), cols(f)], sib_send.at[0], sib_recv.at[0], (b, sib))
     send_n(series_ref, 0, slice(None), has_n)
     send_m(series_ref, 0, slice(None), has_m)
@@ -373,8 +374,8 @@
     first_core, second_core = both(ordinary, core == 0), both(ordinary, core == 1)
     for k in range(CHUNKS):
         hand_over(k)
-        if k + 2 < CHUNKS:
-            set_out(k + 2)
+        if k + AHEAD < CHUNKS:
+            set_out(k + AHEAD)
         if k == 0:
             receive(whole.at[pl.ds(0, block), cols(sib)], sib_send.at[0], sib_recv.at[0], (b, sib))
             send_n(whole, 1, cols(sib), has_n)
@@ -674,6 +675,15 @@
             when(condition, copy.wait_send)
 
 
+def settle(*refs):
+    sems = refs[-1]
+    copies = [pltpu.make_async_copy(refs[i], refs[3 + i], sems.at[i]) for i in range(3)]
+    for copy in copies:
+        copy.start()
+    for copy in copies:
+        copy.wait()
+
+
 def per_device(blocks, series, scales, width):
     block, quarter = series.shape
     dims, share, wide = 4 * quarter, block // 4, block + LANE
@@ -685,7 +695,7 @@
     hops = 2 * CHUNKS
     pairs = (4, 1, hops, hops, hops, 4, 2, 6, 6, 4, 14, 2, PIECES, PIECES, 4 * PARTS, PARTS)
     counts = [n for n in pairs for _ in range(2)] + [hops]
-    return pl.pallas_call(
+    tiles = pl.pallas_call(
         functools.partial(tiles_kernel, blocks),
         out_shape=(out, out, out),
         in_specs=[
@@ -732,6 +742,13 @@
             collective_id=0, has_side_effects=True, vmem_limit_bytes=48 * 1024 * 1024
         ),
     )(series, inv, width)
+    return pl.pallas_call(
+        settle,
+        out_shape=(out, out, out),
+        in_specs=[pl.BlockSpec(memory_space=pltpu.VMEM)] * 3,
+        out_specs=(pl.BlockSpec(memory_space=pltpu.HBM),) * 3,
+        scratch_shapes=[pltpu.SemaphoreType.DMA((3,))],
+    )(*tiles)
 
 
 def solution(mesh):

time: 78.5 us -> 83.6 us (1.065)
  Pallas kernels: 72.2 us -> 77.1 us
    pallas_call x0 -> x1, Pallas kernels: none -> 3.54 us  [per_device(): pl.pallas_call(settle, out_shape=(out, out, out), in_specs=[pl.BlockSpec(...]
    pallas_call x1, Pallas kernels: 72.2 us -> 73.5 us  [per_device(): pl.pallas_call(functools.partial(tiles_kernel, blocks), out_shape=(out, o...]
    unnamed x5 -> x8, local copies, waits for them, and re-layouts: 4.14 us -> 4.19 us
where the time goes in v5:
time: 83.6 us; the launch traced here: 83.4 us
  Pallas kernels  77.1 us (92%)
  local copies, waits for them, and re-layouts  4.19 us (5%)
  between operations  1.46 us (2%)
    pallas_call x1, Pallas kernels, per_device(): pl.pallas_call(functools.partial(tiles_kernel, blocks), out_shape=(out, o...  73.5 us
    unnamed x8, local copies, waits for them, and re-layouts  4.19 us
    pallas_call x1, Pallas kernels, per_device(): pl.pallas_call(settle, out_shape=(out, out, out), in_specs=[pl.BlockSpec(...  3.54 us

profile of v5, /device:TPU:1, one launch (start us, length us, event | category | flops | bytes accessed | tf_op | source)
XLA Modules:
  0.0 83.4 jit_solution(15538879657049172774)
XLA Ops:
  1.3 0.7 divide_bitcast_fusion.inv_ref
  2.0 0.0 copy-start.3
  2.0 1.2 %copy-done.3 = bf16[1024,512]{1,0:T(8,128)(2,1)S(1)} copy-done((bf16[1024,512]{1,0:T(8,128)(2,1)S(1)}, bf16[1024,512]{1,0:T(8,128)(2,1)}, u32[]{:S(2)}) %copy-start.3) | copy-done | bytes 1048600
  3.2 73.5 %shard_map.58 = (f32[256,1024]{1,0:T(8,128)S(1)}, f32[256,1024]{1,0:T(8,128)S(1)}, f32[256,1024]{1,0:T(8,128)S(1)}) custom-call(bf16[1024,512]{1,0:T(8,128)(2,1)S(1)} %copy-done.3, f32[8,128]{1,0:T(8,128)S(1)} %divide_bitcast_fusion.inv_ref, f32[1]{0:T(128)S(6)} %copy.6.width_ref), custom_call_target="tpu_custom_call" | custom-call | tf_op jit(solution)/shard_map/pallas_call | solution.py:698
  76.7 0.0 copy-start
  76.7 1.0 %copy-done = f32[256,1024]{1,0:T(8,128)} copy-done((f32[256,1024]{1,0:T(8,128)}, f32[256,1024]{1,0:T(8,128)S(1)}, u32[]{:S(2)}) %copy-start) | copy-done | bytes 1048600
  77.7 0.0 copy-start.1
  77.7 1.0 %copy-done.1 = f32[256,1024]{1,0:T(8,128)} copy-done((f32[256,1024]{1,0:T(8,128)}, f32[256,1024]{1,0:T(8,128)S(1)}, u32[]{:S(2)}) %copy-start.1) | copy-done | bytes 1048600
  78.7 0.0 copy-start.2
  78.7 1.0 %copy-done.2 = f32[256,1024]{1,0:T(8,128)} copy-done((f32[256,1024]{1,0:T(8,128)}, f32[256,1024]{1,0:T(8,128)S(1)}, u32[]{:S(2)}) %copy-start.2) | copy-done | bytes 1048600
  79.7 3.5 %shard_map.59 = (f32[256,1024]{1,0:T(8,128)}, f32[256,1024]{1,0:T(8,128)}, f32[256,1024]{1,0:T(8,128)}) custom-call(f32[256,1024]{1,0:T(8,128)} %copy-done, f32[256,1024]{1,0:T(8,128)} %copy-done.1, f32[256,1024]{1,0:T(8,128)} %copy-done.2), custom_call_target="tpu_custom_call" | custom-call | tf_op jit(solution)/shard_map/pallas_call | solution.py:745
Async XLA Ops:
  2.0 1.2 %copy-start.3 = (bf16[1024,512]{1,0:T(8,128)(2,1)S(1)}, bf16[1024,512]{1,0:T(8,128)(2,1)}, u32[]{:S(2)}) copy-start(bf16[1024,512]{1,0:T(8,128)(2,1)} %series_ref.1) | copy-start | bytes 3145732
  76.7 1.0 %copy-start = (f32[256,1024]{1,0:T(8,128)}, f32[256,1024]{1,0:T(8,128)S(1)}, u32[]{:S(2)}) copy-start(f32[256,1024]{1,0:T(8,128)S(1)} %get-tuple-element.6.refs_0_) | copy-start | bytes 3145732
  77.7 1.0 %copy-start.1 = (f32[256,1024]{1,0:T(8,128)}, f32[256,1024]{1,0:T(8,128)S(1)}, u32[]{:S(2)}) copy-start(f32[256,1024]{1,0:T(8,128)S(1)} %get-tuple-element.7.refs_1_) | copy-start | bytes 3145732
  78.7 1.0 %copy-start.2 = (f32[256,1024]{1,0:T(8,128)}, f32[256,1024]{1,0:T(8,128)S(1)}, u32[]{:S(2)}) copy-start(f32[256,1024]{1,0:T(8,128)S(1)} %get-tuple-element.8.refs_2_) | copy-start | bytes 3145732

commit v6 on v4

--- a/solution.py
+++ b/solution.py
@@ -412,13 +412,13 @@
             send_m(whole, 3, cols(cross), second_core)
             send_n_quarter(2, place_of(2), is_end)
             send_m(whole, 2, cols(far), is_near, (0,))
-            own_group(near_half)
-            add_products(same_gram, rows, near_half, True)
         if k == 5:
             passed(3)
             send_n(whole, 3, cols(cross), second_core)
             send_n_quarter(3, place_of(2), is_end)
             send_m(whole, 3, cols(cross), is_near, (0,))
+            own_group(near_half)
+            add_products(same_gram, rows, near_half, True)
         if k == 6:
             send_n_quarter(2, place_of(4), is_end)
             send_m(whole, 2, cols(far), is_near, (1,))
@@ -474,12 +474,12 @@
     def second_halves(c):
         return [(g * share + part_rows, part_rows) for g in (2 * c, 2 * c + 1)]
 
-    def tile(products_of, target, pick, parts, ready):
+    def tile(products_of, target, pick, parts, ready, summed=False):
         per = target.shape[0] // 32 // parts
         span = target.shape[1] // 2
         for h in range(parts):
             for c in range(2):
-                for t in range(h * per + 1 if h else 0, (h + 1) * per + 1):
+                for t in () if summed else range(h * per + 1 if h else 0, (h + 1) * per + 1):
                     x = with_lead(products_of, pl.ds(t * 32, 40), c)
                     for step in (1, 2, 4):
                         x = x + pltpu.roll(pltpu.roll(x, step, 0), step, 1)
@@ -570,7 +570,7 @@
     upper = pl.ds(0, part_rows)
 
     def rest_of_next():
-        tile(gram, kept_rest, first_halves, 1, lambda h: None)
+        tile(gram, kept_rest, first_halves, 1, lambda h: None, summed=True)
         for s, j, by in hops:
             turned_rest[seconds(j), :] = kept_rest[:, seconds(j)].T
             post(turned_rest.at[seconds(j), :], rest_hop.at[s], rest_hop_send.at[s], rest_hop_recv.at[s], (over, by))

time: 78.5 us -> 78.5 us (level)
  no operation moved by 1% of the time
where the time goes in v6:
time: 78.5 us; the launch traced here: 78.3 us
  Pallas kernels  72.2 us (92%)
  local copies, waits for them, and re-layouts  4.14 us (5%)
  between operations  1.29 us (2%)
    pallas_call x1, Pallas kernels, per_device(): pl.pallas_call(functools.partial(tiles_kernel, blocks), out_shape=(out, o...  72.2 us
    unnamed x5, local copies, waits for them, and re-layouts  4.14 us

profile of v6, /device:TPU:1, one launch (start us, length us, event | category | flops | bytes accessed | tf_op | source)
XLA Modules:
  0.0 78.3 jit_solution(3635512565205282645)
XLA Ops:
  1.3 0.7 divide_bitcast_fusion.inv_ref
  2.0 0.0 copy-start
  2.0 1.2 %copy-done = bf16[1024,512]{1,0:T(8,128)(2,1)S(1)} copy-done((bf16[1024,512]{1,0:T(8,128)(2,1)S(1)}, bf16[1024,512]{1,0:T(8,128)(2,1)}, u32[]{:S(2)}) %copy-start) | copy-done | bytes 1048600
  3.2 72.2 %shard_map.58 = (f32[256,1024]{1,0:T(8,128)S(1)}, f32[256,1024]{1,0:T(8,128)S(1)}, f32[256,1024]{1,0:T(8,128)S(1)}) custom-call(bf16[1024,512]{1,0:T(8,128)(2,1)S(1)} %copy-done, f32[8,128]{1,0:T(8,128)S(1)} %divide_bitcast_fusion.inv_ref, f32[1]{0:T(128)S(6)} %copy.9.width_ref), custom_call_target="tpu_custom_call" | custom-call | tf_op jit(solution)/shard_map/pallas_call | solution.py:688
  75.4 1.0 %copy.10 = f32[256,1024]{1,0:T(8,128)} copy(f32[256,1024]{1,0:T(8,128)S(1)} %get-tuple-element.6) | data formatting | bytes 2097152
  76.3 1.0 %copy.11 = f32[256,1024]{1,0:T(8,128)} copy(f32[256,1024]{1,0:T(8,128)S(1)} %get-tuple-element.7) | data formatting | bytes 2097152
  77.3 1.0 %copy.12 = f32[256,1024]{1,0:T(8,128)} copy(f32[256,1024]{1,0:T(8,128)S(1)} %get-tuple-element.8) | data formatting | bytes 2097152
Async XLA Ops:
  2.0 1.2 %copy-start = (bf16[1024,512]{1,0:T(8,128)(2,1)S(1)}, bf16[1024,512]{1,0:T(8,128)(2,1)}, u32[]{:S(2)}) copy-start(bf16[1024,512]{1,0:T(8,128)(2,1)} %series_ref.1) | copy-start | bytes 3145732

commit v7 on v6

--- a/solution.py
+++ b/solution.py
@@ -265,7 +265,6 @@
             leaves(hop.at[s, k], ride_send.at[i], n_recv.at[0], is_end)
 
     set_out(0)
-    set_out(1)
     send(series_ref, whole.at[pl.ds(0, block), cols(f)], sib_send.at[0], sib_recv.at[0], (b, sib))
     send_n(series_ref, 0, slice(None), has_n)
     send_m(series_ref, 0, slice(None), has_m)
@@ -373,8 +372,8 @@
     first_core, second_core = both(ordinary, core == 0), both(ordinary, core == 1)
     for k in range(CHUNKS):
         hand_over(k)
-        if k + 2 < CHUNKS:
-            set_out(k + 2)
+        if k + 1 < CHUNKS:
+            set_out(k + 1)
         if k == 0:
             receive(whole.at[pl.ds(0, block), cols(sib)], sib_send.at[0], sib_recv.at[0], (b, sib))
             send_n(whole, 1, cols(sib), has_n)

time: 78.5 us -> 90.3 us (1.15)
  Pallas kernels: 72.2 us -> 84 us
    pallas_call x1, Pallas kernels: 72.2 us -> 84 us  [per_device(): pl.pallas_call(functools.partial(tiles_kernel, blocks), out_shape=(out, o...]
where the time goes in v7:
time: 90.3 us; the launch traced here: 90.1 us
  Pallas kernels  84 us (93%)
  local copies, waits for them, and re-layouts  4.14 us (5%)
  between operations  1.29 us (1%)
    pallas_call x1, Pallas kernels, per_device(): pl.pallas_call(functools.partial(tiles_kernel, blocks), out_shape=(out, o...  84 us
    unnamed x5, local copies, waits for them, and re-layouts  4.14 us

profile of v7, /device:TPU:1, one launch (start us, length us, event | category | flops | bytes accessed | tf_op | source)
XLA Modules:
  0.0 90.1 jit_solution(10797625854045494564)
XLA Ops:
  1.3 0.7 divide_bitcast_fusion.inv_ref
  2.0 0.0 copy-start
  2.0 1.2 %copy-done = bf16[1024,512]{1,0:T(8,128)(2,1)S(1)} copy-done((bf16[1024,512]{1,0:T(8,128)(2,1)S(1)}, bf16[1024,512]{1,0:T(8,128)(2,1)}, u32[]{:S(2)}) %copy-start) | copy-done | bytes 1048600
  3.2 84.0 %shard_map.58 = (f32[256,1024]{1,0:T(8,128)S(1)}, f32[256,1024]{1,0:T(8,128)S(1)}, f32[256,1024]{1,0:T(8,128)S(1)}) custom-call(bf16[1024,512]{1,0:T(8,128)(2,1)S(1)} %copy-done, f32[8,128]{1,0:T(8,128)S(1)} %divide_bitcast_fusion.inv_ref, f32[1]{0:T(128)S(6)} %copy.9.width_ref), custom_call_target="tpu_custom_call" | custom-call | tf_op jit(solution)/shard_map/pallas_call | solution.py:687
  87.2 1.0 %copy.10 = f32[256,1024]{1,0:T(8,128)} copy(f32[256,1024]{1,0:T(8,128)S(1)} %get-tuple-element.6) | data formatting | bytes 2097152
  88.2 1.0 %copy.11 = f32[256,1024]{1,0:T(8,128)} copy(f32[256,1024]{1,0:T(8,128)S(1)} %get-tuple-element.7) | data formatting | bytes 2097152
  89.1 1.0 %copy.12 = f32[256,1024]{1,0:T(8,128)} copy(f32[256,1024]{1,0:T(8,128)S(1)} %get-tuple-element.8) | data formatting | bytes 2097152
Async XLA Ops:
  2.0 1.2 %copy-start = (bf16[1024,512]{1,0:T(8,128)(2,1)S(1)}, bf16[1024,512]{1,0:T(8,128)(2,1)}, u32[]{:S(2)}) copy-start(bf16[1024,512]{1,0:T(8,128)(2,1)} %series_ref.1) | copy-start | bytes 3145732
